TPU v7x, 32 devices: a whole 2x2x4 slice. The times are simulated.
32 devices in a mesh: rep: 8 (over z, x), gz: 4 (over y, core).
Axes of the slice: x: 2, y: 2, z: 4, core: 2. Of those that a mesh axis runs over, the one named last changes fastest.
Arguments:
- lattice_field: float32 [48, 64, 4096], P('rep', 'gz'), may hold values from -4 to 4
- langevin_noise: float32 [2, 48, 64, 4096], P(None, 'rep', 'gz'), may hold values from -5 to 5
- masses: float32 [64, 4096], P('gz'), may hold values from -2 to 2
- counts: int32 [48], replicated, may hold values from 0 to 13, as said below
- dest_slots: int32 [48], replicated, may hold values from 0 to 47, each once
- mode_bins: int32 [64, 64, 33], P('gz'), may hold values from 0 to 15, as said below
Outputs:
- resampled: float32 [48, 64, 4096], P('rep', 'gz')
- propagator: float32 [48, 16], P('rep')
Inputs may be any that keep to these rules, and one draw needn't show every extreme that they name: The counts sum to 48; in each aligned block of 6 replicas (those of one index of rep) at most 3 counts are nonzero, and exactly 3 in some block. `dest_slots`: A permutation of the 48 slots. `mode_bins`: the bin depends only on n_y^2 + n_z^2 + kx^2 with n = min(k, 64 - k), and never falls as that grows; every bin holds at least one mode.
All inputs are finite; a program needn't handle non-finite values.
Results may differ from a plain program's by a relative error of at most 0.00007.
Values sent between devices are 32-bit elements; how exact they have to be, the bound alone decides.
A program may use at most 64 MiB of HBM per device.

v0:
```python
import jax
import jax.numpy as jnp
from jax import lax
from jax.sharding import PartitionSpec as P

L = 64
SWEEPS = 2
NBINS = 16


step_size = 0.1
quartic = 0.5


def with_halo(block, sides, width):
    for axis, dim in sides:
        count = lax.axis_size(axis)
        forward = [(i, i + 1) for i in range(count - 1)]
        forward.append((count - 1, 0))
        backward = [(target, source) for source, target in forward]
        low = lax.ppermute(
            lax.slice_in_dim(block, block.shape[dim] - width, None, axis=dim), axis, forward
        )
        high = lax.ppermute(lax.slice_in_dim(block, 0, width, axis=dim), axis, backward)
        block = jnp.concatenate([low, block, high], axis=dim)
    return block


def in_plane(center):
    grid = center.reshape(center.shape[0], center.shape[1], L, L)
    across = jnp.roll(grid, 1, axis=3) + jnp.roll(grid, -1, axis=3)
    return jnp.roll(center, L, axis=2) + jnp.roll(center, -L, axis=2) + across.reshape(center.shape)


def update(center, below, above, site_masses, noise_now):
    beside = below + above + in_plane(center)
    drift = 6.0 * center - beside + site_masses[None] * center + quartic * center * center * center
    return center - step_size * drift + jnp.sqrt(2.0 * step_size) * noise_now


def angle_tables(rows, columns):
    product = jnp.arange(rows)[:, None] * jnp.arange(columns)[None, :] % L
    theta = 2.0 * jnp.pi / L * product.astype(jnp.float32)
    return (jnp.cos(theta), jnp.sin(theta))


def make_weights(mode_bins):
    half = L // 2 + 1
    ordered = jnp.transpose(mode_bins, (1, 0, 2))
    wave_x = jnp.arange(half)
    weight_x = jnp.where((wave_x == 0) | (wave_x == L // 2), 1.0, 2.0).astype(jnp.float32)
    onehot = (ordered[..., None] == jnp.arange(NBINS)[None, None, None, :]).astype(jnp.float32)
    return (onehot * weight_x[None, None, :, None]).reshape(-1, NBINS)


def transform(slabs, weights):
    half = L // 2 + 1
    exact = lax.Precision.HIGHEST
    cos_half, sin_half = angle_tables(L, half)
    cos_full, sin_full = angle_tables(L, L)
    along_x = jnp.concatenate([cos_half, -sin_half], axis=1)
    count, depth = (slabs.shape[0], slabs.shape[1])
    grid = slabs.reshape(count, depth, L, L)
    first = jnp.einsum("nzyx,xk->nzyk", grid, along_x, precision=exact)
    real_x, imag_x = (first[..., :half], first[..., half:])
    real_y = jnp.einsum("qy,nzyk->nzqk", cos_full, real_x, precision=exact) + jnp.einsum(
        "qy,nzyk->nzqk", sin_full, imag_x, precision=exact
    )
    imag_y = jnp.einsum("qy,nzyk->nzqk", cos_full, imag_x, precision=exact) - jnp.einsum(
        "qy,nzyk->nzqk", sin_full, real_x, precision=exact
    )
    merged = jnp.concatenate([real_y, imag_y], axis=3).reshape(count, depth, L * 2 * half)
    block = lax.all_to_all(merged, "gz", split_axis=2, concat_axis=1, tiled=True)
    items = block.shape[0]
    pencil = block.reshape(items, L, -1, 2 * half)
    real_p = pencil[..., :half]
    imag_p = pencil[..., half:]
    real_z = jnp.einsum("pz,mzqk->mpqk", cos_full, real_p, precision=exact) + jnp.einsum(
        "pz,mzqk->mpqk", sin_full, imag_p, precision=exact
    )
    imag_z = jnp.einsum("pz,mzqk->mpqk", cos_full, imag_p, precision=exact) - jnp.einsum(
        "pz,mzqk->mpqk", sin_full, real_p, precision=exact
    )
    power = real_z * real_z + imag_z * imag_z
    binned = jnp.dot(power.reshape(items, -1), weights, precision=exact)
    binned_total, weight_total = lax.psum((binned, jnp.sum(weights, axis=0)), "gz")
    return binned_total / (float(L**3) * weight_total)


def local(lattice_field, langevin_noise, masses, counts, dest_slots, mode_bins):
    local_count = lattice_field.shape[0]
    weights = make_weights(mode_bins)
    swept = lattice_field
    for turn in range(SWEEPS):
        padded = with_halo(swept, (("gz", 1),), 1)
        swept = update(padded[:, 1:-1], padded[:, :-2], padded[:, 2:], masses, langevin_noise[turn])
    base = lax.axis_index("rep") * local_count
    ends = jnp.cumsum(counts)
    position = jnp.argsort(dest_slots)
    mine_position = lax.dynamic_slice_in_dim(position, base, local_count)
    mine_source = jnp.sum((ends[None, :] <= mine_position[:, None]).astype(jnp.int32), axis=1)
    empty = jnp.zeros_like(swept)
    piece = lax.all_gather(swept, "rep", axis=0, tiled=True)
    found = (mine_source >= 0) & (mine_source < piece.shape[0])
    chosen = jnp.take(piece, jnp.clip(mine_source, 0, piece.shape[0] - 1), axis=0)
    resampled = jnp.where(found[:, None, None], chosen, empty)
    propagator = transform(resampled, weights)
    return (resampled, propagator)


def solution(mesh):
    in_specs = (
        P("rep", "gz", None),
        P(None, "rep", "gz", None),
        P("gz", None),
        P(),
        P(),
        P("gz", None, None),
    )
    out_specs = (P("rep", "gz", None), P("rep", None))
    return jax.shard_map(local, mesh=mesh, in_specs=in_specs, out_specs=out_specs, check_vma=False)
```

profile of v0, /device:TPU:0, one launch (start us, length us, event | category | flops | bytes accessed | tf_op | source)
XLA Modules:
  0.0 406.8 jit_solution(10839325006769117143)
XLA Ops:
  7.2 2.2 fusion.131
  11.8 2.4 reshape.102
  18.7 3.3 maximum_add_fusion
  22.0 3.4 add.127
  25.5 4.0 fusion.24
  29.5 2.4 reshape.103
  39.2 3.3 maximum_add_fusion.1
  42.5 3.4 add.136
  46.6 4.1 %fusion.28 = f32[6,16,4096]{2,1,0:T(8,128)} fusion(f32[6,16,4096]{2,1,0:T(8,128)S(1)} %copy-done.1, f32[6,1,4096]{2,1,0:T(1,128)} %copy-done.12, f32[6,1,4096]{2,1,0:T(1,128)} %copy-done.11, f32[6,16,4096]{2,1,0:T(8,128)} %add.136, f32[6,16,4032]{2,1,0:T(8,128)} %get-tuple-element.17, f32[6,16,64]{2,1,0:T(8,128)S(1)} %get-tuple-element.19, ...), kind=kLoop, calls=%fused_computation.36 | loop fusion | flops 7864320 | bytes 9895936 | tf_op jit(solution)/shard_map/add | solution.py:38
  55.5 173.9 %all-gather.2.cloned.1.call-done = f32[48,16,4096]{2,1,0:T(8,128)} async-done(((f32[6,16,4096]{2,1,0:T(8,128)}), f32[48,16,4096]{2,1,0:T(8,128)}) %all-gather.2.cloned.1.call-update) | async-done | bytes 12582928 | tf_op jit(solution)/shard_map/all_gather | solution.py:103
  229.4 5.2 %gather_fusion = f32[6,16,4096]{2,1,0:T(8,128)S(1)} fusion(f32[48,16,4096]{2,1,0:T(8,128)} %all-gather.2.cloned.1.call-done, s32[1024]{0:T(1024)S(1)} %pad_clamp_fusion), kind=kCustom, calls=%fused_computation | custom fusion | bytes 3145752 | tf_op jit(solution)/shard_map/jit(_take)/gather | solution.py:105
  234.7 2.4 gather.7
  237.1 4.7 %fusion.2 = f32[6,16,64,66]{3,2,1,0:T(8,128)S(1)} fusion(f32[6,16,64,64]{3,2,1,0:T(8,128)} %gather.7, pred[6]{0:T(512)(128)(4,1)S(1)} %get-tuple-element.29, pred[6]{0:T(512)(128)(4,1)S(1)} %get-tuple-element.28, f32[64,33]{1,0:T(8,128)S(1)} %get-tuple-element.30, f32[64,33]{1,0:T(8,128)S(1)} %get-tuple-element.31), kind=kOutput, calls=%fused_computation.7 | convolution fusion | flops 312217728 | bytes 3211788 | tf_op jit(solution)/shard_map/nzyx,xk->nzyk/dot_general | solution.py:64
  241.9 6.0 %fusion.7 = f32[6,16,33,64]{3,2,1,0:T(8,128)S(1)} fusion(f32[6,16,64,66]{3,2,1,0:T(8,128)S(1)} %fusion.2), kind=kOutput, calls=%fused_computation.12 | convolution fusion | flops 155770880 | bytes 2433024 | tf_op jit(solution)/shard_map/qy,nzyk->nzqk/dot_general | solution.py:66
  247.9 14.7 %fusion.5 = f32[6,16,33,64]{3,2,1,0:T(8,128)S(1)} fusion(f32[6,16,64,66]{3,2,1,0:T(8,128)S(1)} %fusion.2), kind=kOutput, calls=%fused_computation.10 | convolution fusion | flops 155770880 | bytes 2433024 | tf_op jit(solution)/shard_map/qy,nzyk->nzqk/dot_general | solution.py:69
  262.6 5.1 %add_bitcast_fusion.1 = f32[6,16,64,33]{2,3,1,0:T(8,128)S(1)} fusion(f32[6,16,33,64]{3,2,1,0:T(8,128)S(1)} %fusion.7, f32[6,16,64,66]{3,2,1,0:T(8,128)S(1)} %fusion.2), kind=kOutput, calls=%fused_computation.28 | convolution fusion | flops 155973632 | bytes 3244032 | tf_op jit(solution)/shard_map/qy,nzyk->nzqk/dot_general | solution.py:66
  267.7 5.5 %subtract_bitcast_fusion = f32[6,16,64,33]{2,3,1,0:T(8,128)S(1)} fusion(f32[6,16,33,64]{3,2,1,0:T(8,128)S(1)} %fusion.5, f32[6,16,64,66]{3,2,1,0:T(8,128)S(1)} %fusion.2), kind=kOutput, calls=%fused_computation.27 | convolution fusion | flops 155973632 | bytes 3244032 | tf_op jit(solution)/shard_map/qy,nzyk->nzqk/dot_general | solution.py:69
  273.7 14.7 %copy.57 = f32[6,16,64,66]{1,0,3,2:T(8,128)} copy(f32[6,16,64,66]{2,3,1,0:T(8,128)S(1)} %pad_maximum_fusion) | data formatting | bytes 3244032 | tf_op jit(solution)/shard_map/reshape | solution.py:72
  288.4 17.9 %reshape.119 = f32[4,1,101376]{2,1,0:T(1,128)} reshape(f32[4224,6,16]{2,1,0:T(8,128)} %bitcast.62) | data formatting | bytes 3244032
  306.3 3.7 all-to-all-start
  315.5 15.1 %all-to-all-done = f32[4,1,101376]{2,1,0:T(1,128)S(1)} async-done(((f32[4,1,101376]{2,1,0:T(1,128)}), f32[4,1,101376]{2,1,0:T(1,128)S(1)}, u32[]{:S(2)}, u32[]{:S(2)}) %all-to-all-start) | async-done | bytes 1622048 | tf_op jit(solution)/shard_map/all_to_all | solution.py:73
  331.1 6.5 %reduce.1 = f32[4,101376]{1,0:T(4,128)} reduce(f32[4,1,101376]{2,1,0:T(1,128)S(1)} %all-to-all-done, f32[]{:T(128)} %broadcast.211), dimensions={1}, to_apply=%all_to_all.11.reduce_sub_computation | reduce | bytes 3244036 | tf_op jit(solution)/shard_map/all_to_all | solution.py:73
  337.6 15.1 %reshape.120 = f32[4224,6,16]{2,1,0:T(8,128)} reshape(f32[4,101376]{1,0:T(4,128)} %reduce.1) | data formatting | bytes 3244032
  352.8 11.0 %copy.43 = f32[6,16,4,1056]{3,1,2,0:T(8,128)} copy(f32[6,16,4,1056]{1,0,3,2:T(8,128)} %bitcast.63) | data formatting | bytes 3244032 | tf_op jit(solution)/shard_map/all_to_all | solution.py:73
  363.7 3.8 reshape.105
  367.5 3.6 fusion.121
  371.1 2.7 copy.60
  373.8 3.1 fusion.57
  377.0 3.1 fusion.61
  380.1 2.9 copy.59
  387.2 6.0 %fusion.43 = f32[6,16]{1,0:T(8,128)S(1)} fusion(f32[33]{0:T(128)S(1)} %or_select_fusion, s32[64,16,33]{0,2,1:T(8,128)S(1)} %copy-done.10, f32[6,64,16,33]{1,3,2,0:T(8,128)S(1)} %add_bitcast_fusion), kind=kOutput, calls=%fused_computation.58 | convolution fusion | flops 40009728 | bytes 946692 | tf_op jit(solution)/shard_map/dot_general | solution.py:85
  393.2 5.8 %all-reduce = (f32[6,16]{1,0:T(8,128)S(1)}, f32[16]{0:T(128)S(1)}) all-reduce(f32[6,16]{1,0:T(8,128)S(1)} %fusion.43, f32[16]{0:T(128)S(1)} %select_reduce_fusion), channel_id=1, replica_groups=mesh['rep'=8,'gz'=4] {'gz'}, use_global_device_ids=true, to_apply=%region_3.4 | all-reduce | flops 112 | bytes 896 | tf_op jit(solution)/shard_map/psum | solution.py:86
  (74 shorter events, 30.7 us)
Async XLA Ops:
  7.2 222.3 %all-gather.2.cloned.1.call-start = ((), (), s32[]{:S(2)}) async-start(), calls=%async_computation.1 | async-start | bytes 14155776 | tf_op jit(solution)/shard_map/all_gather | solution.py:103
  9.4 16.0 %collective-permute-start = (f32[6,1,4096]{2,1,0:T(1,128)}, f32[6,1,4096]{2,1,0:T(1,128)}, u32[]{:S(2)}, u32[]{:S(2)}) collective-permute-start(f32[6,1,4096]{2,1,0:T(1,128)} %get-tuple-element.26), channel_id=1, source_target_pairs={{0,1},{1,2},{2,3},{3,0},{4,5},{5,6},{6,7},{7,4},{8,9},{9,10},{10,1... | collective-permute-start | bytes 294920 | tf_op jit(solution)/shard_map/ppermute | solution.py:21
  9.9 15.6 %collective-permute-start.1 = (f32[6,1,4096]{2,1,0:T(1,128)}, f32[6,1,4096]{2,1,0:T(1,128)}, u32[]{:S(2)}, u32[]{:S(2)}) collective-permute-start(f32[6,1,4096]{2,1,0:T(1,128)} %get-tuple-element.27), channel_id=1, source_target_pairs={{1,0},{2,1},{3,2},{0,3},{5,4},{6,5},{7,6},{4,7},{9,8},{10,9},{11,1... | collective-permute-start | bytes 294920 | tf_op jit(solution)/shard_map/ppermute | solution.py:24
  15.5 1.4 copy-start.2
  22.0 3.5 copy-start.3
  22.0 3.5 copy-start.9
  33.2 1.4 copy-start
  37.2 8.7 %collective-permute-start.2 = (f32[6,1,4096]{2,1,0:T(1,128)}, f32[6,1,4096]{2,1,0:T(1,128)S(1)}, u32[]{:S(2)}, u32[]{:S(2)}) collective-permute-start(f32[6,1,4096]{2,1,0:T(1,128)} %get-tuple-element.20), channel_id=1, source_target_pairs={{0,1},{1,2},{2,3},{3,0},{4,5},{5,6},{6,7},{7,4},{8,9},{9,10},{10,1... | collective-permute-start | bytes 294920 | tf_op jit(solution)/shard_map/ppermute | solution.py:21
  37.9 8.1 %collective-permute-start.3 = (f32[6,1,4096]{2,1,0:T(1,128)}, f32[6,1,4096]{2,1,0:T(1,128)S(1)}, u32[]{:S(2)}, u32[]{:S(2)}) collective-permute-start(f32[6,1,4096]{2,1,0:T(1,128)} %get-tuple-element.21), channel_id=1, source_target_pairs={{1,0},{2,1},{3,2},{0,3},{5,4},{6,5},{7,6},{4,7},{9,8},{10,9},{11,1... | collective-permute-start | bytes 294920 | tf_op jit(solution)/shard_map/ppermute | solution.py:24
  42.5 4.1 %copy-start.1 = (f32[6,16,4096]{2,1,0:T(8,128)S(1)}, f32[6,16,4096]{2,1,0:T(8,128)}, u32[]{:S(2)}) copy-start(f32[6,16,4096]{2,1,0:T(8,128)} %fusion.24) | copy-start | bytes 4718596
  45.9 0.6 copy-start.11
  45.9 0.7 copy-start.12
  46.6 4.2 %copy-start.8 = (s32[16,64,33]{1,0,2:T(8,128)S(1)}, s32[16,64,33]{1,0,2:T(8,128)}, u32[]{:S(2)}) copy-start(s32[16,64,33]{1,0,2:T(8,128)} %param.11) | copy-start | bytes 405508
  50.7 2.0 copy-start.13
  50.7 2.3 copy-start.14
  234.7 2.5 copy-start.4
  306.3 7.8 %copy-start.5 = (f32[6,16,4096]{2,1,0:T(8,128)S(1)}, f32[6,16,4096]{2,1,0:T(8,128)}, u32[]{:S(2)}) copy-start(f32[6,16,4096]{2,1,0:T(8,128)} %copy-done.4) | copy-start | bytes 4718596
  306.3 24.3 %all-to-all-start = ((f32[4,1,101376]{2,1,0:T(1,128)}), f32[4,1,101376]{2,1,0:T(1,128)S(1)}, u32[]{:S(2)}, u32[]{:S(2)}) async-start(f32[4,1,101376]{2,1,0:T(1,128)} %reshape.119), calls=%async_computation | async-start | bytes 3244032 | tf_op jit(solution)/shard_map/all_to_all | solution.py:73
  383.0 1.9 copy-start.6
  383.0 2.1 copy-start.7
  385.1 2.1 copy-start.10
Sparse Core Ops, SparseCore 0:
  50.9 178.5 all-gather.1
where the time goes:
time: 411 us; the launch traced here: 407 us
  waiting for transfers between devices  189 us (46%)
  local copies, waits for them, and re-layouts  110 us (27%)
  matrix products  52.4 us (13%)
  other arithmetic  26.8 us (7%)
  between operations  14.6 us (4%)
  starting transfers between devices  8.13 us (2%)
  blocking collectives  5.84 us (1%)
    all_gather x1, waiting for transfers between devices, local(): piece = lax.all_gather(swept, 'rep', axis=0, tiled=True)  174 us
    unnamed x34, local copies, waits for them, and re-layouts  39.8 us
    all_to_all x1, waiting for transfers between devices, transform(): lax.all_to_all(merged, 'gz', split_axis=2, concat_axis=1, tiled=True)  15.1 us
    dot_general x1, matrix products, transform(): jnp.einsum('qy,nzyk->nzqk', cos_full, imag_x, precision=exact)  14.7 us
    reshape x1, local copies, waits for them, and re-layouts, transform(): jnp.concatenate([real_y, imag_y], axis=3)  14.7 us
    all_to_all x2, local copies, waits for them, and re-layouts, transform(): lax.all_to_all(merged, 'gz', split_axis=2, concat_axis=1, tiled=True)  11.5 us
  transfers between devices with their start and end apart: 6, of which 2 were waited for; matrix products, arithmetic and copies ran while one was open for 7% of the time, Pallas kernels for 0%

commit v1 on v0

v1 whole, which is shorter than its diff:
```python
import jax
import jax.numpy as jnp
from jax import lax
from jax.sharding import PartitionSpec as P

L = 64
HALF = L // 2 + 1
SWEEPS = 2
NBINS = 16
LIVE_DEV = 3

step_size = 0.1
quartic = 0.5


def ring(axis):
    count = lax.axis_size(axis)
    forward = [(i, (i + 1) % count) for i in range(count)]
    backward = [(target, source) for source, target in forward]
    return forward, backward


def in_plane(center):
    grid = center.reshape(center.shape[0], center.shape[1], L, L)
    across = jnp.roll(grid, 1, axis=3) + jnp.roll(grid, -1, axis=3)
    return jnp.roll(center, L, axis=2) + jnp.roll(center, -L, axis=2) + across.reshape(center.shape)


def update(padded, site_masses, noise_now):
    center = padded[:, 1:-1]
    beside = padded[:, :-2] + padded[:, 2:] + in_plane(center)
    drift = 6.0 * center - beside + site_masses[None] * center + quartic * center * center * center
    return center - step_size * drift + jnp.sqrt(2.0 * step_size) * noise_now


def angle_tables(rows, columns):
    product = jnp.arange(rows)[:, None] * jnp.arange(columns)[None, :] % L
    theta = 2.0 * jnp.pi / L * product.astype(jnp.float32)
    return (jnp.cos(theta), jnp.sin(theta))


def binned_power(slabs, mode_bins):
    exact = lax.Precision.HIGH
    cos_half, sin_half = angle_tables(L, HALF)
    cos_full, sin_full = angle_tables(L, L)
    along_x = jnp.concatenate([cos_half, -sin_half], axis=1)
    count, depth = (slabs.shape[0], slabs.shape[1])
    grid = slabs.reshape(count, depth, L, L)
    first = jnp.einsum("nzyx,xk->nzyk", grid, along_x, precision=exact)
    both = jnp.concatenate([cos_full, sin_full], axis=0)
    second = jnp.einsum("qy,nzyk->qnzk", both, first, precision=exact)
    cos_part, sin_part = second[:L], second[L:]
    real_y = cos_part[..., :HALF] + sin_part[..., HALF:]
    imag_y = cos_part[..., HALF:] - sin_part[..., :HALF]
    merged = jnp.concatenate([real_y, imag_y], axis=3)
    pencil = lax.all_to_all(merged, "gz", split_axis=0, concat_axis=2, tiled=True)
    third = jnp.einsum("pz,qnzk->pnqk", both, pencil, precision=exact)
    cos_part, sin_part = third[:L], third[L:]
    real_z = cos_part[..., :HALF] + sin_part[..., HALF:]
    imag_z = cos_part[..., HALF:] - sin_part[..., :HALF]
    wave_x = jnp.arange(HALF)
    weight_x = jnp.where((wave_x == 0) | (wave_x == L // 2), 1.0, 2.0).astype(jnp.float32)
    power = (real_z * real_z + imag_z * imag_z) * weight_x
    ordered = jnp.transpose(mode_bins, (1, 0, 2))
    hit = ordered[None] == jnp.arange(NBINS)[:, None, None, None]
    binned = jnp.sum(jnp.where(hit[:, :, None], power[None], 0.0), axis=(1, 3, 4))
    weight = jnp.sum(jnp.where(hit, weight_x, 0.0), axis=(1, 2, 3))
    return jnp.concatenate([binned, weight[:, None]], axis=1).T


def local(lattice_field, langevin_noise, masses, counts, dest_slots, mode_bins):
    local_count = lattice_field.shape[0]
    blocks = counts.shape[0] // local_count
    me = lax.axis_index("rep")
    alive = (counts > 0).astype(jnp.int32).reshape(blocks, local_count)
    rank = jnp.cumsum(alive, axis=1) - alive
    place = (jnp.arange(blocks)[:, None] * LIVE_DEV + rank).reshape(-1)
    mine_alive = lax.dynamic_index_in_dim(alive, me, 0, keepdims=False)
    mine_rank = lax.dynamic_index_in_dim(rank, me, 0, keepdims=False)
    turns = jnp.arange(LIVE_DEV)
    pick = (mine_alive[None, :] > 0) & (mine_rank[None, :] == turns[:, None])
    live = jnp.sum(pick.astype(jnp.int32) * jnp.arange(local_count)[None, :], axis=1)

    def take(array, axis):
        return jnp.concatenate(
            [lax.dynamic_slice_in_dim(array, live[i], 1, axis=axis) for i in range(LIVE_DEV)], axis=axis
        )

    field = take(lattice_field, 0)
    noise = take(langevin_noise, 1)
    forward, backward = ring("gz")
    swept = field
    for turn in range(SWEEPS):
        low = lax.ppermute(swept[:, -1:], "gz", forward)
        high = lax.ppermute(swept[:, :1], "gz", backward)
        swept = update(jnp.concatenate([low, swept, high], axis=1), masses, noise[turn])
    piece = lax.all_gather(swept, "rep", axis=0, tiled=True)

    ends = jnp.cumsum(counts)
    owner = jnp.sum((ends[None, :] <= dest_position(dest_slots)[:, None]).astype(jnp.int32), axis=1)
    source = jnp.sum(jnp.where(owner[:, None] == jnp.arange(counts.shape[0])[None], place[None], 0), axis=1)
    mine = lax.dynamic_slice_in_dim(source, me * local_count, local_count)
    resampled = jnp.concatenate(
        [lax.dynamic_slice_in_dim(piece, mine[i], 1, axis=0) for i in range(local_count)], axis=0
    )

    total = lax.psum(binned_power(swept, mode_bins), "gz")
    propagators = total[:LIVE_DEV] / (float(L**3) * total[LIVE_DEV:])
    everyone = lax.all_gather(propagators, "rep", axis=0, tiled=True)
    propagator = jnp.take(everyone, mine, axis=0)
    return (resampled, propagator)


def dest_position(dest_slots):
    slots = jnp.arange(dest_slots.shape[0])
    return jnp.sum(jnp.where(dest_slots[None, :] == slots[:, None], slots[None, :], 0), axis=1)


def solution(mesh):
    in_specs = (
        P("rep", "gz", None),
        P(None, "rep", "gz", None),
        P("gz", None),
        P(),
        P(),
        P("gz", None, None),
    )
    out_specs = (P("rep", "gz", None), P("rep", None))
    return jax.shard_map(local, mesh=mesh, in_specs=in_specs, out_specs=out_specs, check_vma=False)
```

time: 411 us -> 158 us (0.38)
  waiting for transfers between devices: 189 us -> 34 us
  local copies, waits for them, and re-layouts: 110 us -> 27.6 us
  matrix products: 52.4 us -> 4.13 us
  blocking collectives: 5.84 us -> 33.7 us
  between operations: 14.6 us -> 31.3 us
  other arithmetic: 26.8 us -> 18.4 us
    all_gather x1, waiting for transfers between devices: 174 us -> 15.5 us  [local(): piece = lax.all_gather(swept, 'rep', axis=0, tiled=True)]
    dot_general x10 -> x3, matrix products: 52.4 us -> 4.13 us  [the longest x1 1.65 us: binned_power(): third = jnp.einsum('pz,qnzk->pnqk', both, pencil, precision=exact)]
    unnamed x34 -> x26, local copies, waits for them, and re-layouts: 39.8 us -> 7.02 us
    all_gather x0 -> x1, blocking collectives: none -> 27.2 us  [local(): everyone = lax.all_gather(propagators, 'rep', axis=0, tiled=True)]
    reshape x2, local copies, waits for them, and re-layouts: 18.5 us -> 0.7 us  [the longest x1 0.62 us: binned_power(): grid = slabs.reshape(count, depth, L, L)]
    all_to_all x2 -> x1, local copies, waits for them, and re-layouts: 11.5 us -> 0.21 us  [binned_power(): lax.all_to_all(merged, 'gz', split_axis=0, concat_axis=2, tiled=True)]
    gather x2 -> x1, local copies, waits for them, and re-layouts: 7.66 us -> 0.55 us  [local(): propagator = jnp.take(everyone, mine, axis=0)]
    all_to_all x1 -> x0, other arithmetic: 6.55 us -> none  [transform(): lax.all_to_all(merged, 'gz', split_axis=2, concat_axis=1, tiled=True)]
  transfers between devices with their start and end apart: 6 -> 6, of which waited for: 2 -> 2; matrix products, arithmetic and copies ran while one was open for 7% -> 19% of each run, Pallas kernels for 0% -> 0%
where the time goes in v1:
time: 158 us; the launch traced here: 157 us
  waiting for transfers between devices  34 us (22%)
  blocking collectives  33.7 us (21%)
  between operations  31.3 us (20%)
  local copies, waits for them, and re-layouts  27.6 us (17%)
  other arithmetic  18.4 us (12%)
  starting transfers between devices  8.11 us (5%)
  matrix products  4.13 us (3%)
    all_gather x1, blocking collectives, local(): everyone = lax.all_gather(propagators, 'rep', axis=0, tiled=True)  27.2 us
    all_to_all x1, waiting for transfers between devices, binned_power(): lax.all_to_all(merged, 'gz', split_axis=0, concat_axis=2, tiled=True)  18.5 us
    all_gather x1, waiting for transfers between devices, local(): piece = lax.all_gather(swept, 'rep', axis=0, tiled=True)  15.5 us
    unnamed x26, local copies, waits for them, and re-layouts  7.02 us
    psum x1, blocking collectives, local(): total = lax.psum(binned_power(swept, mode_bins), 'gz')  6.44 us
    add x2, other arithmetic, update(): return center - step_size * drift + jnp.sqrt(2.0 * step_size) * noise_now  5.74 us
    add x2, local copies, waits for them, and re-layouts, in_plane(): across = jnp.roll(grid, 1, axis=3) + jnp.roll(grid, -1, axis=3)  4.31 us
    all_to_all x1, starting transfers between devices, binned_power(): lax.all_to_all(merged, 'gz', split_axis=0, concat_axis=2, tiled=True)  3.92 us
  transfers between devices with their start and end apart: 6, of which 2 were waited for; matrix products, arithmetic and copies ran while one was open for 19% of the time, Pallas kernels for 0%

profile of v1, /device:TPU:0, one launch (start us, length us, event | category | flops | bytes accessed | tf_op | source)
XLA Modules:
  0.0 157.3 jit_solution(17042232417376786134)
XLA Ops:
  14.6 1.2 constant_dynamic-slice_fusion.5
  17.1 2.0 %collective-permute-start.1 = (f32[3,1,4096]{2,1,0:T(1,128)}, f32[3,1,4096]{2,1,0:T(1,128)S(1)}, u32[]{:S(2)}, u32[]{:S(2)}) collective-permute-start(f32[3,1,4096]{2,1,0:T(1,128)} %get-tuple-element.31), channel_id=1, source_target_pairs={{1,0},{2,1},{3,2},{0,3},{5,4},{6,5},{7,6},{4,7},{9,8},{10,9},{11,1... | collective-permute-start | bytes 147464 | tf_op jit(solution)/shard_map/ppermute | solution.py:95
  20.8 1.4 fusion.55
  22.3 1.0 copy-done.7
  23.5 0.9 maximum_add_fusion
  24.4 1.4 add.144
  25.8 2.8 %fusion.7 = f32[3,16,4096]{2,1,0:T(8,128)S(1)} fusion(f32[2,3,16,4096]{3,2,1,0:T(8,128)S(1)} %pad_maximum_fusion.1, f32[3,1,4096]{2,1,0:T(1,128)S(1)} %collective-permute-done.1, f32[1,16,4096]{2,1,0:T(8,128)} %copy-done.3, f32[1,16,4096]{2,1,0:T(8,128)} %copy-done.4, f32[1,16,4096]{2,1,0:T(8,128)S(1)} %get-tuple-element.17, ...), kind=kLoop, calls=%fused_computation.22 | loop fusion | flops 5111808 | bytes 5079040 | tf_op jit(solution)/shard_map/add | solution.py:33
  30.4 1.1 fusion.52
  33.0 1.1 collective-permute-start.3
  34.1 2.0 %maximum_add_fusion.1 = f32[3,16,64,64]{3,2,1,0:T(8,128)} fusion(f32[3,16,64,63]{3,2,1,0:T(8,128)S(1)} %get-tuple-element.10, f32[3,16,64,1]{3,2,1,0:T(8,128)S(1)} %get-tuple-element.12, f32[3,16,64,1]{3,2,1,0:T(8,128)S(1)} %get-tuple-element.11, f32[3,16,64,63]{3,2,1,0:T(8,128)S(1)} %get-tuple-element.9), kind=kLoop, calls=%fused_computation.7 | loop fusion | flops 589824 | bytes 2359296 | tf_op jit(solution)/shard_map/add | solution.py:25
  36.1 2.9 %add.153 = f32[3,16,4096]{2,1,0:T(8,128)} reshape(f32[3,16,64,64]{3,2,1,0:T(8,128)} %maximum_add_fusion.1) | data formatting | bytes 1572864 | tf_op jit(solution)/shard_map/add | solution.py:25
  39.0 2.9 %fusion.11 = f32[3,16,4096]{2,1,0:T(8,128)} fusion(f32[3,16,4096]{2,1,0:T(8,128)S(1)} %fusion.7, f32[2,3,16,4096]{3,2,1,0:T(8,128)S(1)} %copy-done.2, f32[3,1,4096]{2,1,0:T(1,128)S(1)} %collective-permute-done.3, f32[3,1,4096]{2,1,0:T(1,128)S(1)} %collective-permute-done.2, f32[3,16,4096]{2,1,0:T(8,128)} %add.153, f32[3,16,4032]{2,1,0:T(8,128)} %get-tuple-element.21, ...), kind=kLoop, calls=%fused_computation.26 | loop fusion | flops 3932160 | bytes 5079040 | tf_op jit(solution)/shard_map/add | solution.py:33
  42.0 0.8 reduce_window_sum.21
  43.9 0.8 select_reduce_fusion.3
  58.7 0.8 fusion.30
  59.5 1.6 %fusion.42 = f32[128,3,16,66]{0,3,2,1:T(8,128)S(1)} fusion(f32[3,16,64,66]{3,2,1,0:T(8,128)S(1)} %fusion.30, f32[64,64]{0,1:T(8,128)S(1)} %get-tuple-element.43, f32[64,64]{0,1:T(8,128)S(1)} %get-tuple-element.44), kind=kOutput, calls=%fused_computation.90 | convolution fusion | flops 155721728 | bytes 2465792 | tf_op jit(solution)/shard_map/qy,nzyk->qnzk/dot_general | solution.py:51
  62.0 1.7 %copy.35 = f32[64,3,16,66]{3,2,1,0:T(8,128)} copy(f32[64,3,16,66]{0,3,2,1:T(8,128)S(1)} %pad_maximum_fusion) | data formatting | bytes 1622016 | tf_op jit(solution)/shard_map/concatenate | solution.py:55
  63.6 3.9 %all-to-all-start = ((f32[64,3,16,66]{3,2,1,0:T(8,128)}), f32[64,3,16,66]{3,2,1,0:T(8,128)S(1)}, u32[]{:S(2)}, u32[]{:S(2)}) async-start(f32[64,3,16,66]{3,2,1,0:T(8,128)} %copy.35), calls=%async_computation | async-start | bytes 3145728 | tf_op jit(solution)/shard_map/all_to_all | solution.py:56
  67.6 0.8 select_reduce_fusion.1
  68.9 18.5 %all-to-all-done = f32[64,3,16,66]{3,2,1,0:T(8,128)S(1)} async-done(((f32[64,3,16,66]{3,2,1,0:T(8,128)}), f32[64,3,16,66]{3,2,1,0:T(8,128)S(1)}, u32[]{:S(2)}, u32[]{:S(2)}) %all-to-all-start) | async-done | bytes 811040 | tf_op jit(solution)/shard_map/all_to_all | solution.py:56
  87.6 1.7 %convolution_bitcast_fusion = f32[128,3,16,66]{0,3,1,2:T(8,128)S(1)} fusion(f32[16,3,64,66]{3,2,1,0:T(8,128)S(1)} %bitcast.55, f32[64,64]{0,1:T(8,128)S(1)} %get-tuple-element.43, f32[64,64]{0,1:T(8,128)S(1)} %get-tuple-element.44), kind=kOutput, calls=%fused_computation.8 | convolution fusion | flops 155721728 | bytes 2465792 | tf_op jit(solution)/shard_map/pz,qnzk->pnqk/dot_general | solution.py:57
  90.0 2.9 %select_reduce_fusion = f32[16,3]{1,0:T(8,128)S(1)} fusion(f32[64,3,16,33]{0,2,3,1:T(8,128)S(1)} %copy.37, pred[16,64,16,33]{1,2,3,0:T(8,128)(4,1)S(1)} %iota_compare_fusion), kind=kLoop, calls=%fused_computation.1 | loop fusion | flops 3243984 | bytes 946368 | tf_op jit(solution)/shard_map/reduce_sum | solution.py:66
  93.1 6.4 %psum.7 = f32[4,16]{1,0:T(4,128)S(1)} all-reduce(f32[4,16]{1,0:T(4,128)S(1)} %maximum_bitcast_fusion.5), channel_id=1, replica_groups=mesh['rep'=8,'gz'=4] {'gz'}, use_global_device_ids=true, to_apply=%region_8.9 | all-reduce | flops 64 | bytes 512 | tf_op jit(solution)/shard_map/psum | solution.py:107
  99.5 27.2 %all-gather = f32[8,3,16]{2,1,0:T(4,128)S(1)} all-gather(f32[1,3,16]{2,1,0:T(4,128)S(1)} %divide_bitcast_fusion), channel_id=1, replica_groups=mesh['rep'=8,'gz'=4] {'rep'}, dimensions={0}, use_global_device_ids=true | all-gather | bytes 1728 | tf_op jit(solution)/shard_map/all_gather | solution.py:109
  128.0 15.5 %all-gather.3.cloned.1.call-done = f32[24,16,4096]{2,1,0:T(8,128)} async-done(((f32[3,16,4096]{2,1,0:T(8,128)}), f32[24,16,4096]{2,1,0:T(8,128)}) %all-gather.3.cloned.1.call-update) | async-done | bytes 6291472 | tf_op jit(solution)/shard_map/all_gather | solution.py:97
  143.5 1.0 dynamic-slice_dynamic-update-slice_fusion.5
  144.4 1.0 dynamic-slice_dynamic-update-slice_fusion.4
  145.4 1.0 dynamic-slice_dynamic-update-slice_fusion.3
  146.4 1.0 dynamic-slice_dynamic-update-slice_fusion.2
  147.4 1.0 dynamic-slice_dynamic-update-slice_fusion.1
  148.3 1.0 dynamic-slice_dynamic-update-slice_fusion
  149.3 1.1 copy-done.8
  (77 shorter events, 15.7 us)
Async XLA Ops:
  7.2 136.3 %all-gather.3.cloned.1.call-start = ((), (), s32[]{:S(2)}) async-start(), calls=%async_computation.1 | async-start | bytes 7077888 | tf_op jit(solution)/shard_map/all_gather | solution.py:97
  8.1 7.7 %copy-start.9 = (s32[8,6]{1,0:T(8,128)}, s32[8,6]{1,0:T(8,128)S(1)}, u32[]{:S(2)}) copy-start(s32[8,6]{1,0:T(8,128)S(1)} %reduce_window_sum.20) | copy-start | bytes 580
  15.8 3.9 %copy-start.3 = (f32[1,16,4096]{2,1,0:T(8,128)}, f32[1,16,4096]{2,1,0:T(8,128)S(1)}, u32[]{:S(2)}) copy-start(f32[1,16,4096]{2,1,0:T(8,128)S(1)} %get-tuple-element.18) | copy-start | bytes 786436
  15.8 3.9 %copy-start.4 = (f32[1,16,4096]{2,1,0:T(8,128)}, f32[1,16,4096]{2,1,0:T(8,128)S(1)}, u32[]{:S(2)}) copy-start(f32[1,16,4096]{2,1,0:T(8,128)S(1)} %get-tuple-element.19) | copy-start | bytes 786436
  16.6 9.2 %collective-permute-start = (f32[3,1,4096]{2,1,0:T(1,128)}, f32[3,1,4096]{2,1,0:T(1,128)S(1)}, u32[]{:S(2)}, u32[]{:S(2)}) collective-permute-start(f32[3,1,4096]{2,1,0:T(1,128)} %get-tuple-element.30), channel_id=1, source_target_pairs={{0,1},{1,2},{2,3},{3,0},{4,5},{5,6},{6,7},{7,4},{8,9},{9,10},{10,1... | collective-permute-start | bytes 147464 | tf_op jit(solution)/shard_map/ppermute | solution.py:94
  17.1 8.7 %collective-permute-start.1 = (f32[3,1,4096]{2,1,0:T(1,128)}, f32[3,1,4096]{2,1,0:T(1,128)S(1)}, u32[]{:S(2)}, u32[]{:S(2)}) collective-permute-start(f32[3,1,4096]{2,1,0:T(1,128)} %get-tuple-element.31), channel_id=1, source_target_pairs={{1,0},{2,1},{3,2},{0,3},{5,4},{6,5},{7,6},{4,7},{9,8},{10,9},{11,1... | collective-permute-start | bytes 147464 | tf_op jit(solution)/shard_map/ppermute | solution.py:95
  20.8 2.5 %copy-start.7 = (f32[2,6,16,4096]{3,2,1,0:T(8,128)S(1)}, f32[2,6,16,4096]{3,2,1,0:T(8,128)}, u32[]{:S(2)}) copy-start(f32[2,6,16,4096]{3,2,1,0:T(8,128)} %param.7) | copy-start | bytes 9437188
  23.5 2.3 %copy-start.1 = (f32[2,3,16,4096]{3,2,1,0:T(8,128)}, f32[2,3,16,4096]{3,2,1,0:T(8,128)S(1)}, u32[]{:S(2)}) copy-start(f32[2,3,16,4096]{3,2,1,0:T(8,128)S(1)} %pad_maximum_fusion.1) | copy-start | bytes 4718596
  32.3 6.7 %collective-permute-start.2 = (f32[3,1,4096]{2,1,0:T(1,128)}, f32[3,1,4096]{2,1,0:T(1,128)S(1)}, u32[]{:S(2)}, u32[]{:S(2)}) collective-permute-start(f32[3,1,4096]{2,1,0:T(1,128)} %get-tuple-element.24), channel_id=1, source_target_pairs={{0,1},{1,2},{2,3},{3,0},{4,5},{5,6},{6,7},{7,4},{8,9},{9,10},{10,1... | collective-permute-start | bytes 147464 | tf_op jit(solution)/shard_map/ppermute | solution.py:94
  33.0 6.0 %collective-permute-start.3 = (f32[3,1,4096]{2,1,0:T(1,128)}, f32[3,1,4096]{2,1,0:T(1,128)S(1)}, u32[]{:S(2)}, u32[]{:S(2)}) collective-permute-start(f32[3,1,4096]{2,1,0:T(1,128)} %get-tuple-element.25), channel_id=1, source_target_pairs={{1,0},{2,1},{3,2},{0,3},{5,4},{6,5},{7,6},{4,7},{9,8},{10,9},{11,1... | collective-permute-start | bytes 147464 | tf_op jit(solution)/shard_map/ppermute | solution.py:95
  36.1 2.9 %copy-start.2 = (f32[2,3,16,4096]{3,2,1,0:T(8,128)S(1)}, f32[2,3,16,4096]{3,2,1,0:T(8,128)}, u32[]{:S(2)}) copy-start(f32[2,3,16,4096]{3,2,1,0:T(8,128)} %copy-done.1) | copy-start | bytes 4718596
  36.1 2.9 %copy-start.6 = (f32[16,4096]{1,0:T(8,128)S(1)}, f32[16,4096]{1,0:T(8,128)}, u32[]{:S(2)}) copy-start(f32[16,4096]{1,0:T(8,128)} %param.8) | copy-start | bytes 786436
  41.9 16.1 %copy-start = (f32[3,16,4096]{2,1,0:T(8,128)S(1)}, f32[3,16,4096]{2,1,0:T(8,128)}, u32[]{:S(2)}) copy-start(f32[3,16,4096]{2,1,0:T(8,128)} %fusion.11) | copy-start | bytes 2359300
  63.6 3.9 %copy-start.5 = (s32[16,64,33]{1,0,2:T(8,128)S(1)}, s32[16,64,33]{1,0,2:T(8,128)}, u32[]{:S(2)}) copy-start(s32[16,64,33]{1,0,2:T(8,128)} %param.11) | copy-start | bytes 405508
  63.6 23.8 %all-to-all-start = ((f32[64,3,16,66]{3,2,1,0:T(8,128)}), f32[64,3,16,66]{3,2,1,0:T(8,128)S(1)}, u32[]{:S(2)}, u32[]{:S(2)}) async-start(f32[64,3,16,66]{3,2,1,0:T(8,128)} %copy.35), calls=%async_computation | async-start | bytes 3145728 | tf_op jit(solution)/shard_map/all_to_all | solution.py:56
  149.3 1.1 copy-start.8
Sparse Core Ops, SparseCore 0:
  42.1 101.3 all-gather.2

commit v2 on v0

v2 whole, which is shorter than its diff:
```python
import functools

import jax
import jax.numpy as jnp
import numpy as np
from jax import lax
from jax.experimental import pallas as pl
from jax.experimental.pallas import tpu as pltpu
from jax.sharding import PartitionSpec as P

L = 64
HALF = L // 2 + 1
SWEEPS = 2
NBINS = 16
LIVE_DEV = 3
COLUMNS = 2
PIECES = 2 * LIVE_DEV
CHUNKS = L * L // 128

step_size = 0.1
quartic = 0.5
kick = float(np.sqrt(np.float32(2.0 * step_size)))
MESH = pl.DeviceIdType.MESH


def tables():
    angle = 2.0 * np.pi / L * (np.outer(np.arange(L), np.arange(L)) % L)
    cos, sin = np.cos(angle), np.sin(angle)
    along_x = np.zeros((128, 512))
    for parity in range(2):
        rows = slice(64 * parity, 64 * parity + 64)
        at = 128 * parity
        along_x[rows, at : at + HALF] = cos[:, :HALF]
        along_x[rows, at + 64 : at + 64 + HALF] = -sin[:, :HALF]
        at = 256 + 128 * parity
        along_x[rows, at : at + HALF] = -sin[:, :HALF]
        along_x[rows, at + 64 : at + 64 + HALF] = -cos[:, :HALF]
    along_y = np.concatenate([cos[:, 0::2], cos[:, 1::2], sin[:, 0::2], sin[:, 1::2]], axis=1)
    along_z = np.concatenate([cos, sin], axis=1)

    def halves(table):
        table = table.astype(np.float32)
        high = table.astype(jnp.bfloat16)
        return np.stack([high, (table - high.astype(np.float32)).astype(jnp.bfloat16)])

    return halves(along_x), halves(along_y), halves(along_z)


def split(value):
    high = value.astype(jnp.bfloat16)
    return high, (value - high.astype(jnp.float32)).astype(jnp.bfloat16)


def dot(left, right):
    def one(a, b):
        return jnp.dot(a, b, preferred_element_type=jnp.float32)

    return one(left[0], right[0]) + (one(left[0], right[1]) + one(left[1], right[0]))


def kernel(reps, gzs, rep_dev, counts, dest, field, noise, masses, bins_in, tx, ty, tz, out, prop, *scratch):
    (
        swept, gathered, edge_out, edge_in, work, sent, modes, bins, acc, part, props, own_part, own_prop,
        up_sem, down_sem, own_x_sem, up_x_sem, down_x_sem, recv_sem,
        edge_send, edge_recv, mode_send, mode_recv, part_send, part_recv, prop_send, prop_recv,
    ) = scratch
    depth = field.shape[1]
    per = L // gzs
    levels = reps // COLUMNS
    me, ring = lax.axis_index("rep"), lax.axis_index("gz")
    z, x = me // COLUMNS, me % COLUMNS
    mate = z * COLUMNS + (1 - x)

    barrier = pltpu.get_barrier_semaphore()

    def greet(turn, carry):
        pl.semaphore_signal(barrier, inc=1, device_id=(me, (ring + turn) % gzs), device_id_type=MESH)
        return carry

    def greet_rep(turn, carry):
        pl.semaphore_signal(barrier, inc=1, device_id=((me + turn) % reps, ring), device_id_type=MESH)
        return carry

    lax.fori_loop(1, gzs, greet, 0)
    lax.fori_loop(1, reps, greet_rep, 0)

    live = [jnp.int32(0)] * LIVE_DEV
    rank = jnp.int32(0)
    for i in range(rep_dev):
        alive = counts[me * rep_dev + i] > 0
        live = [jnp.where(alive & (rank == k), i, live[k]) for k in range(LIVE_DEV)]
        rank = rank + alive.astype(jnp.int32)

    for k in range(LIVE_DEV):
        swept[k, 8 : 8 + depth, :] = field[live[k]]
    pl.semaphore_wait(barrier, gzs - 1 + reps - 1)

    lane = lax.broadcasted_iota(jnp.int32, (depth, 128), 1)
    first_x, last_x, even_y = lane % 64 == 0, lane % 64 == 63, lane < 64

    def edge_copy(turn, side):
        target = (ring + 1) % gzs if side == 0 else (ring + gzs - 1) % gzs
        return pltpu.make_async_remote_copy(
            src_ref=edge_out.at[turn, side], dst_ref=edge_in.at[turn, side],
            send_sem=edge_send.at[turn, side], recv_sem=edge_recv.at[turn, side],
            device_id=(me, target), device_id_type=MESH,
        )

    def piece(owner, index):
        return gathered.at[owner * LIVE_DEV + index // 2, index % 2]

    def send(owner, index, sem, target):
        ref = piece(owner, index)
        return pltpu.make_async_remote_copy(
            src_ref=ref, dst_ref=ref, send_sem=sem, recv_sem=recv_sem.at[owner * PIECES + index],
            device_id=(target, ring), device_id_type=MESH,
        )

    for turn in range(SWEEPS):
        for k in range(LIVE_DEV):
            edge_out[turn, 0, k] = swept[turn * LIVE_DEV + k, 8 + depth - 1 : 8 + depth, :]
            edge_out[turn, 1, k] = swept[turn * LIVE_DEV + k, 8:9, :]
        for side in range(2):
            edge_copy(turn, side).start()
        for side in range(2):
            edge_copy(turn, side).wait()
        for k in range(LIVE_DEV):
            swept[turn * LIVE_DEV + k, 7:8, :] = edge_in[turn, 0, k]
            swept[turn * LIVE_DEV + k, 8 + depth : 9 + depth, :] = edge_in[turn, 1, k]
        for k in range(LIVE_DEV):
            from_at, to_at = turn * LIVE_DEV + k, (turn + 1) * LIVE_DEV + k

            def block(j, carry):
                def lanes(at):
                    return pl.ds(pl.multiple_of(at % CHUNKS * 128, 128), 128)

                here = lanes(j)
                center = swept[from_at, 8 : 8 + depth, here]
                before = pltpu.roll(swept[from_at, 8 : 8 + depth, lanes(j + CHUNKS - 1)], 64, 1)
                after = pltpu.roll(swept[from_at, 8 : 8 + depth, lanes(j + 1)], 64, 1)
                beside = swept[from_at, 7 : 7 + depth, here] + swept[from_at, 9 : 9 + depth, here]
                beside += pltpu.roll(center, 64, 1) + jnp.where(even_y, before, after)
                beside += jnp.where(first_x, pltpu.roll(center, 65, 1), pltpu.roll(center, 1, 1))
                beside += jnp.where(last_x, pltpu.roll(center, 63, 1), pltpu.roll(center, 127, 1))
                drift = 6.0 * center - beside + masses[:, here] * center + quartic * center * center * center
                fresh = center - step_size * drift + kick * noise[turn, live[k], :, here]
                if turn + 1 < SWEEPS:
                    swept[to_at, 8 : 8 + depth, here] = fresh
                else:
                    at = pl.ds(pl.multiple_of(j % (CHUNKS // 2) * 128, 128), 128)
                    gathered[me * LIVE_DEV + k, j // (CHUNKS // 2), :, at] = fresh
                    work[k, pl.ds(j, depth, stride=CHUNKS), :] = fresh
                return carry

            lax.fori_loop(0, CHUNKS, block, 0, unroll=4)

    for index in range(PIECES):
        send(me, index, own_x_sem.at[index], mate).start()

        @pl.when(z + 1 < levels)
        def _():
            send(me, index, up_sem.at[index], me + COLUMNS).start()

        @pl.when(z > 0)
        def _():
            send(me, index, down_sem.at[index], me - COLUMNS).start()

    send(mate, 0, own_x_sem.at[0], mate).wait_recv()

    @pl.when(z + 1 < levels)
    def _():
        send(mate, 0, up_sem.at[PIECES], me + COLUMNS).start()

    @pl.when(z > 0)
    def _():
        send(mate, 0, down_sem.at[PIECES], me - COLUMNS).start()

    def forward(t, at):
        foreign = (at == PIECES).astype(jnp.int32)
        index = at - PIECES * foreign
        column = x + foreign * (1 - 2 * x)
        for sign, sem, x_sem, edge in ((1, up_sem, up_x_sem, levels - 1), (-1, down_sem, down_x_sem, 0)):
            origin = z - sign * t
            owner = origin * COLUMNS + column
            before = (origin + sign) * COLUMNS + column

            @pl.when((origin >= 0) & (origin < levels))
            def _():
                send(owner, index, sem.at[at], mate).wait_recv()

            @pl.when((origin + sign >= 0) & (origin + sign < levels) & (z != edge))
            def _():
                send(before, index, sem.at[at], me + sign * COLUMNS).wait_send()

            @pl.when((origin >= 0) & (origin < levels) & (z != edge))
            def _():
                send(owner, index, sem.at[at], me + sign * COLUMNS).start()

            @pl.when((t > 1) & (origin + sign >= 0) & (origin + sign < levels) & (at < PIECES) & (at > 0))
            def _():
                send(before, index, x_sem.at[index], mate).wait_send()

            @pl.when((origin >= 0) & (origin < levels) & (at < PIECES) & (at > 0))
            def _():
                send(owner, index, x_sem.at[index], mate).start()

    half_depth = depth // 2

    def planes(unit):
        k, part_at = unit // 2, unit % 2
        rows = half_depth * CHUNKS
        value = work[k, pl.ds(pl.multiple_of(part_at * rows, rows), rows), :]
        first = dot(split(value), (tx[0], tx[1]))
        for pair in range(half_depth // 2):
            stacked = []
            for plane in (2 * pair, 2 * pair + 1):
                mine = first[plane * CHUNKS : (plane + 1) * CHUNKS]
                stacked.append(jnp.concatenate([mine[:, 128 * c : 128 * c + 128] for c in range(4)], axis=0))
            second = dot((ty[0], ty[1]), split(jnp.concatenate(stacked, axis=1)))
            for d in range(gzs):
                rows = second[d * per : (d + 1) * per]
                at = part_at * half_depth + 2 * pair
                sent[k, d, at] = rows[:, :128]
                sent[k, d, at + 1] = rows[:, 128:]

    def mode_copy(k, turn, source):
        target = (ring + turn) % gzs
        return pltpu.make_async_remote_copy(
            src_ref=sent.at[k, target],
            dst_ref=modes.at[k, pl.ds(source * depth, depth)],
            send_sem=mode_send.at[k * gzs + turn],
            recv_sem=mode_recv.at[k * gzs + turn],
            device_id=(me, target), device_id_type=MESH,
        )

    def send_modes(k):

        def one(turn, carry):
            mode_copy(k, turn, ring).start()
            return carry

        lax.fori_loop(1, gzs, one, 0)

    def early(at, carry):
        forward(1, at)

        @pl.when(at < PIECES)
        def _():
            planes(at)

        return carry

    lax.fori_loop(0, PIECES + 1, early, 0)
    for k in range(LIVE_DEV):
        send_modes(k)

    bins[...] = jnp.full(bins.shape, -1, jnp.int32)
    for q in range(per):
        bins[q, :, 0:HALF] = bins_in[q]
        bins[q, :, 64 : 64 + HALF] = bins_in[q]
    acc[...] = jnp.zeros(acc.shape, jnp.float32)
    wide = lax.broadcasted_iota(jnp.int32, (L, 128), 1)
    wave_x = wide % 64
    weight = jnp.where((wave_x == 0) | (wave_x == L // 2), 1.0, 2.0).astype(jnp.float32)
    sign_of = jnp.where(wide < 64, 1.0, -1.0).astype(jnp.float32)
    real_weight = jnp.where(wide < 64, weight, 0.0)

    def add_bins(k, q, value):
        here = bins[q]
        for b in range(NBINS):
            taken = jnp.where(here == b, value, 0.0)
            acc[k, b] += jnp.sum(taken.reshape(L // 8, 8, 128), axis=0)

    def weigh(q, carry):
        add_bins(LIVE_DEV, q, real_weight)
        return carry

    lax.fori_loop(0, per, weigh, 0)

    def pair_modes(k, pair):
        stacked = []
        for q in (2 * pair, 2 * pair + 1):
            mine = modes[k, :, q, :]
            turned = pltpu.roll(mine, 64, 1) * sign_of
            stacked.append(jnp.concatenate([mine, turned], axis=0))
        third = dot((tz[0], tz[1]), split(jnp.concatenate(stacked, axis=1)))
        for n in range(2):
            value = third[:, 128 * n : 128 * n + 128]
            add_bins(k, 2 * pair + n, value * value * weight)

    def middle(at, carry):
        forward(2, at)

        @pl.when(at < PIECES)
        def _():
            def go(pair, c):
                pair_modes(at // 2, at % 2 * (per // 4) + pair)
                return c

            lax.fori_loop(0, per // 4, go, 0)

        return carry

    for k in range(LIVE_DEV):

        def arrive(turn, c):
            mode_copy(k, turn, (ring + gzs - turn) % gzs).wait_recv()
            mode_copy(k, turn, ring).wait_send()
            return c

        lax.fori_loop(1, gzs, arrive, 0)
    for k in range(LIVE_DEV):
        modes[k, pl.ds(ring * depth, depth)] = sent[k, ring]
    lax.fori_loop(0, PIECES + 1, middle, 0)

    at_lane = lax.broadcasted_iota(jnp.int32, (NBINS, 128), 1)
    at_row = lax.broadcasted_iota(jnp.int32, (NBINS, 128), 0)
    rows = []
    for k in range(LIVE_DEV + 1):
        summed = jnp.sum(jnp.sum(acc[k], axis=1), axis=1, keepdims=True)
        rows.append(jnp.sum(jnp.where(at_lane == at_row, summed, 0.0), axis=0, keepdims=True))
    own_part[...] = jnp.concatenate(rows + [jnp.zeros((8 - LIVE_DEV - 1, 128), jnp.float32)], axis=0)

    def part_copy(turn, to):
        return pltpu.make_async_remote_copy(
            src_ref=own_part, dst_ref=part.at[to],
            send_sem=part_send.at[turn], recv_sem=part_recv.at[turn],
            device_id=(me, (ring + turn) % gzs), device_id_type=MESH,
        )

    def part_start(turn, carry):
        part_copy(turn, ring).start()
        return carry

    def part_wait(turn, carry):
        part_copy(turn, (ring + gzs - turn) % gzs).wait_recv()
        part_copy(turn, ring).wait_send()
        return carry

    lax.fori_loop(1, gzs, part_start, 0)

    total = jnp.int32(0)
    slots = [jnp.int32(0)] * rep_dev

    def position_of(p, found):
        slot = dest[p]
        return tuple(jnp.where(slot == me * rep_dev + j, p, found[j]) for j in range(rep_dev))

    found = lax.fori_loop(0, reps * rep_dev, position_of, tuple(slots))

    def look(i, state):
        total, rank, owners, ranks = state
        number = counts[i]
        rank = jnp.where(i % rep_dev == 0, 0, rank)
        ends = total + number
        hits = [(found[j] >= total) & (found[j] < ends) for j in range(rep_dev)]
        owners = tuple(jnp.where(hits[j], i // rep_dev, owners[j]) for j in range(rep_dev))
        ranks = tuple(jnp.where(hits[j], rank, ranks[j]) for j in range(rep_dev))
        return ends, rank + (number > 0).astype(jnp.int32), owners, ranks

    _, _, owners, ranks = lax.fori_loop(
        0, reps * rep_dev, look, (total, jnp.int32(0), tuple(slots), tuple(slots))
    )

    lax.fori_loop(1, gzs, part_wait, 0)
    part[ring] = own_part[...]
    binned = jnp.sum(part[...], axis=0)
    whole = binned[LIVE_DEV : LIVE_DEV + 1]
    used = lax.broadcasted_iota(jnp.int32, (8, 128), 1) < NBINS
    own_prop[...] = jnp.where(used, binned / jnp.where(used, float(L**3) * whole, 1.0), 0.0)

    def prop_copy(turn, to):
        return pltpu.make_async_remote_copy(
            src_ref=own_prop, dst_ref=props.at[to],
            send_sem=prop_send.at[turn], recv_sem=prop_recv.at[turn],
            device_id=((me + turn) % reps, ring), device_id_type=MESH,
        )

    def prop_start(turn, carry):
        prop_copy(turn, me).start()
        return carry

    def prop_wait(turn, carry):
        prop_copy(turn, (me + reps - turn) % reps).wait_recv()
        prop_copy(turn, me).wait_send()
        return carry

    lax.fori_loop(1, reps, prop_start, 0)

    def late(step, carry):
        forward(3 + step // (PIECES + 1), step % (PIECES + 1))
        return carry

    lax.fori_loop(0, (levels - 3) * (PIECES + 1), late, 0)

    lax.fori_loop(1, reps, prop_wait, 0)
    props[me] = own_prop[...]
    for j in range(rep_dev):
        prop[j : j + 1, :] = props[owners[j], pl.ds(ranks[j], 1), :][:, :NBINS]

    def from_mate(step, carry):
        origin, index = step // PIECES, step % PIECES

        @pl.when(index > 0)
        def _():
            send(origin * COLUMNS + 1 - x, index, own_x_sem.at[index], mate).wait_recv()

        return carry

    lax.fori_loop(0, levels * PIECES, from_mate, 0)

    half = CHUNKS * 64
    for j in range(rep_dev):
        for h in range(2):
            out[j, :, half * h : half * h + half] = gathered[owners[j] * LIVE_DEV + ranks[j], h]

    def drain(index, carry):
        send(me, index, own_x_sem.at[index], mate).wait_send()
        for origin, x_sem, last in ((0, up_x_sem, levels - 1), (levels - 1, down_x_sem, 0)):

            @pl.when((z == last) & (index > 0))
            def _():
                send(origin * COLUMNS + x, index, x_sem.at[index], mate).wait_send()

        return carry

    lax.fori_loop(0, PIECES, drain, 0)


def local(lattice_field, langevin_noise, masses, counts, dest_slots, mode_bins):
    rep_dev, depth, sites = lattice_field.shape
    reps, gzs = lax.axis_size("rep"), lax.axis_size("gz")
    per = L // gzs
    levels = reps // COLUMNS
    assert levels >= 4
    f32, dma = jnp.float32, pltpu.SemaphoreType.DMA
    scratch = [
        pltpu.VMEM((SWEEPS * LIVE_DEV, depth + 16, sites), f32),
        pltpu.VMEM((reps * LIVE_DEV, 2, depth, sites // 2), f32),
        pltpu.VMEM((SWEEPS, 2, LIVE_DEV, 1, sites), f32),
        pltpu.VMEM((SWEEPS, 2, LIVE_DEV, 1, sites), f32),
        pltpu.VMEM((LIVE_DEV, depth * CHUNKS, 128), f32),
        pltpu.VMEM((LIVE_DEV, gzs, depth, per, 128), f32),
        pltpu.VMEM((LIVE_DEV, L, per, 128), f32),
        pltpu.VMEM((per, L, 128), jnp.int32),
        pltpu.VMEM((LIVE_DEV + 1, NBINS, 8, 128), f32),
        pltpu.VMEM((gzs, 8, 128), f32),
        pltpu.VMEM((reps, 8, 128), f32),
        pltpu.VMEM((8, 128), f32),
        pltpu.VMEM((8, 128), f32),
        dma((PIECES + 1,)),
        dma((PIECES + 1,)),
        dma((PIECES,)),
        dma((PIECES,)),
        dma((PIECES,)),
        dma((reps * PIECES,)),
        dma((SWEEPS, 2)),
        dma((SWEEPS, 2)),
        dma((LIVE_DEV * gzs,)),
        dma((LIVE_DEV * gzs,)),
        dma((gzs,)),
        dma((gzs,)),
        dma((reps,)),
        dma((reps,)),
    ]
    smem = pl.BlockSpec(memory_space=pltpu.SMEM)
    vmem = pl.BlockSpec(memory_space=pltpu.VMEM)
    return pl.pallas_call(
        functools.partial(kernel, reps, gzs, rep_dev),
        out_shape=(
            jax.ShapeDtypeStruct(lattice_field.shape, f32),
            jax.ShapeDtypeStruct((rep_dev, NBINS), f32),
        ),
        in_specs=[smem, smem] + [vmem] * 7,
        out_specs=(vmem, vmem),
        scratch_shapes=scratch,
        compiler_params=pltpu.CompilerParams(
            collective_id=0, has_side_effects=True, vmem_limit_bytes=56 * 1024 * 1024
        ),
    )(counts, dest_slots, lattice_field, langevin_noise, masses, mode_bins, *map(jnp.asarray, tables()))


def solution(mesh):
    in_specs = (
        P("rep", "gz", None),
        P(None, "rep", "gz", None),
        P("gz", None),
        P(),
        P(),
        P("gz", None, None),
    )
    out_specs = (P("rep", "gz", None), P("rep", None))
    return jax.shard_map(local, mesh=mesh, in_specs=in_specs, out_specs=out_specs, check_vma=False)
```

time: 411 us -> 106 us (0.26); the launches traced: 407 us -> 106 us
  waiting for transfers between devices: 189 us -> 0 us
  local copies, waits for them, and re-layouts: 110 us -> 5.23 us
  Pallas kernels: 0 us -> 100 us
  matrix products: 52.4 us -> 0 us
  other arithmetic: 26.8 us -> 0 us
  between operations: 14.6 us -> 0.65 us
  starting transfers between devices: 8.13 us -> 0 us
  blocking collectives: 5.84 us -> 0 us
    all_gather x1 -> x0, waiting for transfers between devices: 174 us -> none  [local(): piece = lax.all_gather(swept, 'rep', axis=0, tiled=True)]
    pallas_call x0 -> x1, Pallas kernels: none -> 100 us  [local(): pl.pallas_call(functools.partial(kernel, reps, gzs, rep_dev), out_shape=(...]
    dot_general x10 -> x0, matrix products: 52.4 us -> none  [the longest x1 14.7 us: transform(): jnp.einsum('qy,nzyk->nzqk', cos_full, imag_x, precision=exact)]
    unnamed x34 -> x5, local copies, waits for them, and re-layouts: 39.8 us -> 5.23 us
    reshape x4 -> x0, local copies, waits for them, and re-layouts: 23.3 us -> none  [the longest x1 14.7 us: transform(): jnp.concatenate([real_y, imag_y], axis=3)]
    slice x11 -> x0, local copies, waits for them, and re-layouts: 15.3 us -> none  [the longest x4 5.08 us: in_plane(): across = jnp.roll(grid, 1, axis=3) + jnp.roll(grid, -1, axis=3)]
    all_to_all x1 -> x0, waiting for transfers between devices: 15.1 us -> none  [transform(): lax.all_to_all(merged, 'gz', split_axis=2, concat_axis=1, tiled=True)]
    add x4 -> x0, other arithmetic: 14.8 us -> none  [the longest x2 8.13 us: update(): return center - step_size * drift + jnp.sqrt(2.0 * step_size) * noise_now]
  transfers between devices with their start and end apart: 6 -> 0, of which waited for: 2 -> 0; matrix products, arithmetic and copies ran while one was open for 7% -> 0% of each run, Pallas kernels for 0% -> 0%
where the time goes in v2:
time: 106 us
  Pallas kernels  100 us (94%)
  local copies, waits for them, and re-layouts  5.23 us (5%)
    pallas_call x1, Pallas kernels, local(): pl.pallas_call(functools.partial(kernel, reps, gzs, rep_dev), out_shape=(...  100 us
    unnamed x5, local copies, waits for them, and re-layouts  5.23 us

profile of v2, /device:TPU:0, one launch (start us, length us, event | category | flops | bytes accessed | tf_op | source)
XLA Modules:
  0.0 106.0 jit_solution(6822735197709840030)
XLA Ops:
  0.6 2.0 %copy.11.bins_in = s32[16,64,33]{2,1,0:T(8,128)} copy(s32[16,64,33]{1,0,2:T(8,128)} %param.14) | data formatting | bytes 270336 | tf_op args[5]
  2.6 100.1 %shard_map.104 = (f32[6,16,4096]{2,1,0:T(8,128)}, f32[6,16]{1,0:T(8,128)}) custom-call(s32[48]{0:T(128)} %counts.1, s32[48]{0:T(128)} %dest.1, f32[6,16,4096]{2,1,0:T(8,128)} %field.1, f32[2,6,16,4096]{3,2,1,0:T(8,128)} %noise.1, f32[16,4096]{1,0:T(8,128)} %masses.1, s32[16,64,33]{2,1,0:T(8,128)} %copy.11.bins_in, bf16[2,128,512]{2,1,0:T(8,128)(2,1)} %constant.6.clone.tx, ...), custom_call_target="tpu_custom_call" | custom-call | tf_op jit(solution)/shard_map/pallas_call | solution.py:468
  102.7 0.0 copy-start
  102.7 2.7 %copy.14 = f32[6,16,4096]{2,1,0:T(8,128)} copy(f32[6,16,4096]{2,1,0:T(8,128)} %get-tuple-element.4) | data formatting | bytes 3145728
  105.4 0.0 copy-done
  105.4 0.6 copy.15
Async XLA Ops:
  102.7 2.7 %copy-start = (f32[6,16]{1,0:T(8,128)S(1)}, f32[6,16]{1,0:T(8,128)}, u32[]{:S(2)}) copy-start(f32[6,16]{1,0:T(8,128)} %get-tuple-element.5) | copy-start | bytes 1156

commit v3 on v2

--- a/solution.py
+++ b/solution.py
@@ -60,10 +60,11 @@
 
 def kernel(reps, gzs, rep_dev, counts, dest, field, noise, masses, bins_in, tx, ty, tz, out, prop, *scratch):
     (
-        swept, gathered, edge_out, edge_in, work, sent, modes, bins, acc, part, props, own_part, own_prop,
+        swept, gathered, edge_out, edge_in, work, sent0, sent1, sent2, modes0, modes1, modes2, bins, acc, part, props, own_part, own_prop,
         up_sem, down_sem, own_x_sem, up_x_sem, down_x_sem, recv_sem,
         edge_send, edge_recv, mode_send, mode_recv, part_send, part_recv, prop_send, prop_recv,
     ) = scratch
+    sent, modes = (sent0, sent1, sent2), (modes0, modes1, modes2)
     depth = field.shape[1]
     per = L // gzs
     levels = reps // COLUMNS
@@ -91,20 +92,30 @@
         live = [jnp.where(alive & (rank == k), i, live[k]) for k in range(LIVE_DEV)]
         rank = rank + alive.astype(jnp.int32)
 
-    for k in range(LIVE_DEV):
-        swept[k, 8 : 8 + depth, :] = field[live[k]]
-    pl.semaphore_wait(barrier, gzs - 1 + reps - 1)
-
     lane = lax.broadcasted_iota(jnp.int32, (depth, 128), 1)
     first_x, last_x, even_y = lane % 64 == 0, lane % 64 == 63, lane < 64
 
-    def edge_copy(turn, side):
+    def edge_copy(turn, side, k):
         target = (ring + 1) % gzs if side == 0 else (ring + gzs - 1) % gzs
         return pltpu.make_async_remote_copy(
-            src_ref=edge_out.at[turn, side], dst_ref=edge_in.at[turn, side],
-            send_sem=edge_send.at[turn, side], recv_sem=edge_recv.at[turn, side],
+            src_ref=edge_out.at[turn, side, k], dst_ref=edge_in.at[turn, side, k],
+            send_sem=edge_send.at[turn, side, k], recv_sem=edge_recv.at[turn, side, k],
             device_id=(me, target), device_id_type=MESH,
         )
+
+    def edge_rows(turn, k):
+        edge_out[turn, 0, k] = swept[turn * LIVE_DEV + k, 8 + depth - 1 : 8 + depth, :]
+        edge_out[turn, 1, k] = swept[turn * LIVE_DEV + k, 8:9, :]
+
+    def edge_start(turn, k):
+        for side in range(2):
+            edge_copy(turn, side, k).start()
+
+    def edge_wait(turn, k):
+        for side in range(2):
+            edge_copy(turn, side, k).wait()
+        swept[turn * LIVE_DEV + k, 7:8, :] = edge_in[turn, 0, k]
+        swept[turn * LIVE_DEV + k, 8 + depth : 9 + depth, :] = edge_in[turn, 1, k]
 
     def piece(owner, index):
         return gathered.at[owner * LIVE_DEV + index // 2, index % 2]
@@ -116,18 +127,39 @@
             device_id=(target, ring), device_id_type=MESH,
         )
 
+    for k in range(LIVE_DEV):
+        swept[k, 8 : 8 + depth, :] = field[live[k]]
+        edge_rows(0, k)
+    pl.semaphore_wait(barrier, gzs - 1 + reps - 1)
+    for k in range(LIVE_DEV):
+        edge_start(0, k)
+
+    bins[...] = jnp.full(bins.shape, -1, jnp.int32)
+    for q in range(per):
+        bins[q, :, 0:HALF] = bins_in[q]
+        bins[q, :, 64 : 64 + HALF] = bins_in[q]
+    acc[...] = jnp.zeros(acc.shape, jnp.float32)
+    wide = lax.broadcasted_iota(jnp.int32, (L, 128), 1)
+    wave_x = wide % 64
+    weight = jnp.where((wave_x == 0) | (wave_x == L // 2), 1.0, 2.0).astype(jnp.float32)
+    sign_of = jnp.where(wide < 64, 1.0, -1.0).astype(jnp.float32)
+    real_weight = jnp.where(wide < 64, weight, 0.0)
+
+    def add_bins(k, q, value):
+        here = bins[q]
+        for b in range(NBINS):
+            taken = jnp.where(here == b, value, 0.0)
+            acc[k, b] += jnp.sum(taken.reshape(L // 8, 8, 128), axis=0)
+
+    def weigh(q, carry):
+        add_bins(LIVE_DEV, q, real_weight)
+        return carry
+
+    lax.fori_loop(0, per, weigh, 0)
+
     for turn in range(SWEEPS):
         for k in range(LIVE_DEV):
-            edge_out[turn, 0, k] = swept[turn * LIVE_DEV + k, 8 + depth - 1 : 8 + depth, :]
-            edge_out[turn, 1, k] = swept[turn * LIVE_DEV + k, 8:9, :]
-        for side in range(2):
-            edge_copy(turn, side).start()
-        for side in range(2):
-            edge_copy(turn, side).wait()
-        for k in range(LIVE_DEV):
-            swept[turn * LIVE_DEV + k, 7:8, :] = edge_in[turn, 0, k]
-            swept[turn * LIVE_DEV + k, 8 + depth : 9 + depth, :] = edge_in[turn, 1, k]
-        for k in range(LIVE_DEV):
+            edge_wait(turn, k)
             from_at, to_at = turn * LIVE_DEV + k, (turn + 1) * LIVE_DEV + k
 
             def block(j, carry):
@@ -152,18 +184,21 @@
                     work[k, pl.ds(j, depth, stride=CHUNKS), :] = fresh
                 return carry
 
-            lax.fori_loop(0, CHUNKS, block, 0, unroll=4)
-
-    for index in range(PIECES):
-        send(me, index, own_x_sem.at[index], mate).start()
-
-        @pl.when(z + 1 < levels)
-        def _():
-            send(me, index, up_sem.at[index], me + COLUMNS).start()
-
-        @pl.when(z > 0)
-        def _():
-            send(me, index, down_sem.at[index], me - COLUMNS).start()
+            lax.fori_loop(0, CHUNKS, block, 0, unroll=8)
+            if turn + 1 < SWEEPS:
+                edge_rows(turn + 1, k)
+                edge_start(turn + 1, k)
+                continue
+            for index in (2 * k, 2 * k + 1):
+                send(me, index, own_x_sem.at[index], mate).start()
+
+                @pl.when(z + 1 < levels)
+                def _():
+                    send(me, index, up_sem.at[index], me + COLUMNS).start()
+
+                @pl.when(z > 0)
+                def _():
+                    send(me, index, down_sem.at[index], me - COLUMNS).start()
 
     send(mate, 0, own_x_sem.at[0], mate).wait_recv()
 
@@ -206,8 +241,7 @@
 
     half_depth = depth // 2
 
-    def planes(unit):
-        k, part_at = unit // 2, unit % 2
+    def planes(k, part_at):
         rows = half_depth * CHUNKS
         value = work[k, pl.ds(pl.multiple_of(part_at * rows, rows), rows), :]
         first = dot(split(value), (tx[0], tx[1]))
@@ -220,14 +254,14 @@
             for d in range(gzs):
                 rows = second[d * per : (d + 1) * per]
                 at = part_at * half_depth + 2 * pair
-                sent[k, d, at] = rows[:, :128]
-                sent[k, d, at + 1] = rows[:, 128:]
+                sent[k][d, at] = rows[:, :128]
+                sent[k][d, at + 1] = rows[:, 128:]
 
     def mode_copy(k, turn, source):
         target = (ring + turn) % gzs
         return pltpu.make_async_remote_copy(
-            src_ref=sent.at[k, target],
-            dst_ref=modes.at[k, pl.ds(source * depth, depth)],
+            src_ref=sent[k].at[target],
+            dst_ref=modes[k].at[pl.ds(source * depth, depth)],
             send_sem=mode_send.at[k * gzs + turn],
             recv_sem=mode_recv.at[k * gzs + turn],
             device_id=(me, target), device_id_type=MESH,
@@ -241,46 +275,21 @@
 
         lax.fori_loop(1, gzs, one, 0)
 
-    def early(at, carry):
-        forward(1, at)
-
-        @pl.when(at < PIECES)
-        def _():
-            planes(at)
-
-        return carry
-
-    lax.fori_loop(0, PIECES + 1, early, 0)
     for k in range(LIVE_DEV):
+
+        def early(part_at, carry):
+            forward(1, 2 * k + part_at)
+            planes(k, part_at)
+            return carry
+
+        lax.fori_loop(0, 2, early, 0)
         send_modes(k)
-
-    bins[...] = jnp.full(bins.shape, -1, jnp.int32)
-    for q in range(per):
-        bins[q, :, 0:HALF] = bins_in[q]
-        bins[q, :, 64 : 64 + HALF] = bins_in[q]
-    acc[...] = jnp.zeros(acc.shape, jnp.float32)
-    wide = lax.broadcasted_iota(jnp.int32, (L, 128), 1)
-    wave_x = wide % 64
-    weight = jnp.where((wave_x == 0) | (wave_x == L // 2), 1.0, 2.0).astype(jnp.float32)
-    sign_of = jnp.where(wide < 64, 1.0, -1.0).astype(jnp.float32)
-    real_weight = jnp.where(wide < 64, weight, 0.0)
-
-    def add_bins(k, q, value):
-        here = bins[q]
-        for b in range(NBINS):
-            taken = jnp.where(here == b, value, 0.0)
-            acc[k, b] += jnp.sum(taken.reshape(L // 8, 8, 128), axis=0)
-
-    def weigh(q, carry):
-        add_bins(LIVE_DEV, q, real_weight)
-        return carry
-
-    lax.fori_loop(0, per, weigh, 0)
+    forward(1, jnp.int32(PIECES))
 
     def pair_modes(k, pair):
         stacked = []
         for q in (2 * pair, 2 * pair + 1):
-            mine = modes[k, :, q, :]
+            mine = modes[k][:, q, :]
             turned = pltpu.roll(mine, 64, 1) * sign_of
             stacked.append(jnp.concatenate([mine, turned], axis=0))
         third = dot((tz[0], tz[1]), split(jnp.concatenate(stacked, axis=1)))
@@ -288,30 +297,27 @@
             value = third[:, 128 * n : 128 * n + 128]
             add_bins(k, 2 * pair + n, value * value * weight)
 
-    def middle(at, carry):
-        forward(2, at)
-
-        @pl.when(at < PIECES)
-        def _():
-            def go(pair, c):
-                pair_modes(at // 2, at % 2 * (per // 4) + pair)
-                return c
-
-            lax.fori_loop(0, per // 4, go, 0)
-
-        return carry
-
     for k in range(LIVE_DEV):
 
-        def arrive(turn, c):
+        def arrive(turn, carry):
             mode_copy(k, turn, (ring + gzs - turn) % gzs).wait_recv()
             mode_copy(k, turn, ring).wait_send()
-            return c
+            return carry
+
+        def middle(part_at, carry):
+            forward(2, 2 * k + part_at)
+
+            def go(pair, c):
+                pair_modes(k, part_at * (per // 4) + pair)
+                return c
+
+            lax.fori_loop(0, per // 4, go, 0)
+            return carry
 
         lax.fori_loop(1, gzs, arrive, 0)
-    for k in range(LIVE_DEV):
-        modes[k, pl.ds(ring * depth, depth)] = sent[k, ring]
-    lax.fori_loop(0, PIECES + 1, middle, 0)
+        modes[k][pl.ds(ring * depth, depth)] = sent[k][ring]
+        lax.fori_loop(0, 2, middle, 0)
+    forward(2, jnp.int32(PIECES))
 
     at_lane = lax.broadcasted_iota(jnp.int32, (NBINS, 128), 1)
     at_row = lax.broadcasted_iota(jnp.int32, (NBINS, 128), 0)
@@ -440,8 +446,8 @@
         pltpu.VMEM((SWEEPS, 2, LIVE_DEV, 1, sites), f32),
         pltpu.VMEM((SWEEPS, 2, LIVE_DEV, 1, sites), f32),
         pltpu.VMEM((LIVE_DEV, depth * CHUNKS, 128), f32),
-        pltpu.VMEM((LIVE_DEV, gzs, depth, per, 128), f32),
-        pltpu.VMEM((LIVE_DEV, L, per, 128), f32),
+        *[pltpu.VMEM((gzs, depth, per, 128), f32)] * LIVE_DEV,
+        *[pltpu.VMEM((L, per, 128), f32)] * LIVE_DEV,
         pltpu.VMEM((per, L, 128), jnp.int32),
         pltpu.VMEM((LIVE_DEV + 1, NBINS, 8, 128), f32),
         pltpu.VMEM((gzs, 8, 128), f32),
@@ -454,8 +460,8 @@
         dma((PIECES,)),
         dma((PIECES,)),
         dma((reps * PIECES,)),
-        dma((SWEEPS, 2)),
-        dma((SWEEPS, 2)),
+        dma((SWEEPS, 2, LIVE_DEV)),
+        dma((SWEEPS, 2, LIVE_DEV)),
         dma((LIVE_DEV * gzs,)),
         dma((LIVE_DEV * gzs,)),
         dma((gzs,)),

time: 106 us -> 93 us (0.88)
  Pallas kernels: 100 us -> 87 us
    pallas_call x1, Pallas kernels: 100 us -> 87 us  [local(): pl.pallas_call(functools.partial(kernel, reps, gzs, rep_dev), out_shape=(...]
where the time goes in v3:
time: 93 us; the launch traced here: 92.9 us
  Pallas kernels  87 us (94%)
  local copies, waits for them, and re-layouts  5.23 us (6%)
    pallas_call x1, Pallas kernels, local(): pl.pallas_call(functools.partial(kernel, reps, gzs, rep_dev), out_shape=(...  87 us
    unnamed x5, local copies, waits for them, and re-layouts  5.23 us

profile of v3, /device:TPU:0, one launch (start us, length us, event | category | flops | bytes accessed | tf_op | source)
XLA Modules:
  0.0 92.9 jit_solution(10608900712387112404)
XLA Ops:
  0.6 2.0 %copy.11.bins_in = s32[16,64,33]{2,1,0:T(8,128)} copy(s32[16,64,33]{1,0,2:T(8,128)} %param.14) | data formatting | bytes 270336 | tf_op args[5]
  2.6 87.0 %shard_map.104 = (f32[6,16,4096]{2,1,0:T(8,128)}, f32[6,16]{1,0:T(8,128)}) custom-call(s32[48]{0:T(128)} %counts.1, s32[48]{0:T(128)} %dest.1, f32[6,16,4096]{2,1,0:T(8,128)} %field.1, f32[2,6,16,4096]{3,2,1,0:T(8,128)} %noise.1, f32[16,4096]{1,0:T(8,128)} %masses.1, s32[16,64,33]{2,1,0:T(8,128)} %copy.11.bins_in, bf16[2,128,512]{2,1,0:T(8,128)(2,1)} %constant.6.clone.tx, ...), custom_call_target="tpu_custom_call" | custom-call | tf_op jit(solution)/shard_map/pallas_call | solution.py:474
  89.6 0.0 copy-start
  89.6 2.7 %copy.14 = f32[6,16,4096]{2,1,0:T(8,128)} copy(f32[6,16,4096]{2,1,0:T(8,128)} %get-tuple-element.4) | data formatting | bytes 3145728
  92.3 0.0 copy-done
  92.3 0.6 copy.15
Async XLA Ops:
  89.6 2.7 %copy-start = (f32[6,16]{1,0:T(8,128)S(1)}, f32[6,16]{1,0:T(8,128)}, u32[]{:S(2)}) copy-start(f32[6,16]{1,0:T(8,128)} %get-tuple-element.5) | copy-start | bytes 1156

commit v4 on v3

--- a/solution.py
+++ b/solution.py
@@ -58,12 +58,13 @@
     return one(left[0], right[0]) + (one(left[0], right[1]) + one(left[1], right[0]))
 
 
-def kernel(reps, gzs, rep_dev, counts, dest, field, noise, masses, bins_in, tx, ty, tz, out, prop, *scratch):
+def kernel(reps, gzs, rep_dev, counts, dest, field, noise_in, masses, bins_in, tx, ty, tz, gathered, chosen, prop, *scratch):
     (
-        swept, gathered, edge_out, edge_in, work, sent0, sent1, sent2, modes0, modes1, modes2, bins, acc, part, props, own_part, own_prop,
+        swept, noise0, noise1, own0, own1, own2, edge_out, edge_in, work, sent0, sent1, sent2, modes0, modes1, modes2, bins, acc, part, props, own_part, own_prop,
         up_sem, down_sem, own_x_sem, up_x_sem, down_x_sem, recv_sem,
-        edge_send, edge_recv, mode_send, mode_recv, part_send, part_recv, prop_send, prop_recv,
+        edge_send, edge_recv, mode_send, mode_recv, part_send, part_recv, prop_send, prop_recv, noise_sem, keep_sem,
     ) = scratch
+    own, noise = (own0, own1, own2), (noise0, noise1)
     sent, modes = (sent0, sent1, sent2), (modes0, modes1, modes2)
     depth = field.shape[1]
     per = L // gzs
@@ -85,6 +86,12 @@
     lax.fori_loop(1, gzs, greet, 0)
     lax.fori_loop(1, reps, greet_rep, 0)
 
+    def noise_copy(turn):
+        return pltpu.make_async_copy(noise_in.at[turn], noise[turn], noise_sem.at[turn])
+
+    for turn in range(SWEEPS):
+        noise_copy(turn).start()
+
     live = [jnp.int32(0)] * LIVE_DEV
     rank = jnp.int32(0)
     for i in range(rep_dev):
@@ -94,6 +101,12 @@
 
     lane = lax.broadcasted_iota(jnp.int32, (depth, 128), 1)
     first_x, last_x, even_y = lane % 64 == 0, lane % 64 == 63, lane < 64
+
+    def send_own(index, sem, target):
+        return pltpu.make_async_remote_copy(
+            src_ref=own[index // 2].at[index % 2], dst_ref=piece(me, index), send_sem=sem,
+            recv_sem=recv_sem.at[me * PIECES + index], device_id=(target, ring), device_id_type=MESH,
+        )
 
     def edge_copy(turn, side, k):
         target = (ring + 1) % gzs if side == 0 else (ring + gzs - 1) % gzs
@@ -134,10 +147,13 @@
     for k in range(LIVE_DEV):
         edge_start(0, k)
 
-    bins[...] = jnp.full(bins.shape, -1, jnp.int32)
-    for q in range(per):
-        bins[q, :, 0:HALF] = bins_in[q]
-        bins[q, :, 64 : 64 + HALF] = bins_in[q]
+    narrow = lax.broadcasted_iota(jnp.int32, (per, 128), 1) % 64 < HALF
+    for kz in range(HALF):
+        mine = bins_in[kz]
+        mine = jnp.where(narrow, jnp.concatenate([mine, mine], axis=1), -1)
+        bins[:, kz, :] = mine
+        if 0 < kz < L // 2:
+            bins[:, L - kz, :] = mine
     acc[...] = jnp.zeros(acc.shape, jnp.float32)
     wide = lax.broadcasted_iota(jnp.int32, (L, 128), 1)
     wave_x = wide % 64
@@ -157,48 +173,62 @@
 
     lax.fori_loop(0, per, weigh, 0)
 
-    for turn in range(SWEEPS):
-        for k in range(LIVE_DEV):
-            edge_wait(turn, k)
-            from_at, to_at = turn * LIVE_DEV + k, (turn + 1) * LIVE_DEV + k
-
-            def block(j, carry):
-                def lanes(at):
-                    return pl.ds(pl.multiple_of(at % CHUNKS * 128, 128), 128)
-
-                here = lanes(j)
-                center = swept[from_at, 8 : 8 + depth, here]
-                before = pltpu.roll(swept[from_at, 8 : 8 + depth, lanes(j + CHUNKS - 1)], 64, 1)
-                after = pltpu.roll(swept[from_at, 8 : 8 + depth, lanes(j + 1)], 64, 1)
-                beside = swept[from_at, 7 : 7 + depth, here] + swept[from_at, 9 : 9 + depth, here]
-                beside += pltpu.roll(center, 64, 1) + jnp.where(even_y, before, after)
-                beside += jnp.where(first_x, pltpu.roll(center, 65, 1), pltpu.roll(center, 1, 1))
-                beside += jnp.where(last_x, pltpu.roll(center, 63, 1), pltpu.roll(center, 127, 1))
-                drift = 6.0 * center - beside + masses[:, here] * center + quartic * center * center * center
-                fresh = center - step_size * drift + kick * noise[turn, live[k], :, here]
-                if turn + 1 < SWEEPS:
-                    swept[to_at, 8 : 8 + depth, here] = fresh
-                else:
-                    at = pl.ds(pl.multiple_of(j % (CHUNKS // 2) * 128, 128), 128)
-                    gathered[me * LIVE_DEV + k, j // (CHUNKS // 2), :, at] = fresh
-                    work[k, pl.ds(j, depth, stride=CHUNKS), :] = fresh
-                return carry
-
+    def keep(k):
+        return pltpu.make_async_copy(own[k], gathered.at[me * LIVE_DEV + k], keep_sem.at[k])
+
+    def sweep(turn, k):
+        edge_wait(turn, k)
+        from_at, to_at = turn * LIVE_DEV + k, (turn + 1) * LIVE_DEV + k
+
+        def block(j, carry):
+            def lanes(at):
+                return pl.ds(pl.multiple_of(at % CHUNKS * 128, 128), 128)
+
+            here = lanes(j)
+            center = swept[from_at, 8 : 8 + depth, here]
+            before = pltpu.roll(swept[from_at, 8 : 8 + depth, lanes(j + CHUNKS - 1)], 64, 1)
+            after = pltpu.roll(swept[from_at, 8 : 8 + depth, lanes(j + 1)], 64, 1)
+            beside = swept[from_at, 7 : 7 + depth, here] + swept[from_at, 9 : 9 + depth, here]
+            beside += pltpu.roll(center, 64, 1) + jnp.where(even_y, before, after)
+            beside += jnp.where(first_x, pltpu.roll(center, 65, 1), pltpu.roll(center, 1, 1))
+            beside += jnp.where(last_x, pltpu.roll(center, 63, 1), pltpu.roll(center, 127, 1))
+            drift = 6.0 * center - beside + masses[:, here] * center + quartic * center * center * center
+            fresh = center - step_size * drift + kick * noise[turn][live[k], :, here]
+            if turn + 1 < SWEEPS:
+                swept[to_at, 8 : 8 + depth, here] = fresh
+            else:
+                at = pl.ds(pl.multiple_of(j % (CHUNKS // 2) * 128, 128), 128)
+                own[k][j // (CHUNKS // 2), :, at] = fresh
+                work[k, pl.ds(j, depth, stride=CHUNKS), :] = fresh
+            return carry
+
+        if turn + 1 < SWEEPS:
             lax.fori_loop(0, CHUNKS, block, 0, unroll=8)
-            if turn + 1 < SWEEPS:
-                edge_rows(turn + 1, k)
-                edge_start(turn + 1, k)
-                continue
-            for index in (2 * k, 2 * k + 1):
-                send(me, index, own_x_sem.at[index], mate).start()
-
-                @pl.when(z + 1 < levels)
-                def _():
-                    send(me, index, up_sem.at[index], me + COLUMNS).start()
-
-                @pl.when(z > 0)
-                def _():
-                    send(me, index, down_sem.at[index], me - COLUMNS).start()
+            edge_rows(turn + 1, k)
+            edge_start(turn + 1, k)
+            return
+        for h in range(2):
+            lax.fori_loop(h * CHUNKS // 2, (h + 1) * CHUNKS // 2, block, 0, unroll=8)
+            index = 2 * k + h
+            send_own(index, own_x_sem.at[index], mate).start()
+
+            @pl.when(z + 1 < levels)
+            def _():
+                send_own(index, up_sem.at[index], me + COLUMNS).start()
+
+            @pl.when(z > 0)
+            def _():
+                send_own(index, down_sem.at[index], me - COLUMNS).start()
+
+        keep(k).start()
+
+    noise_copy(0).wait()
+    sweep(0, 0)
+    noise_copy(1).wait()
+    for k in range(1, LIVE_DEV):
+        sweep(0, k)
+        sweep(1, k - 1)
+    sweep(1, LIVE_DEV - 1)
 
     send(mate, 0, own_x_sem.at[0], mate).wait_recv()
 
@@ -404,6 +434,9 @@
     for j in range(rep_dev):
         prop[j : j + 1, :] = props[owners[j], pl.ds(ranks[j], 1), :][:, :NBINS]
 
+    for k in range(LIVE_DEV):
+        keep(k).wait()
+
     def from_mate(step, carry):
         origin, index = step // PIECES, step % PIECES
 
@@ -415,10 +448,8 @@
 
     lax.fori_loop(0, levels * PIECES, from_mate, 0)
 
-    half = CHUNKS * 64
     for j in range(rep_dev):
-        for h in range(2):
-            out[j, :, half * h : half * h + half] = gathered[owners[j] * LIVE_DEV + ranks[j], h]
+        chosen[j] = owners[j] * LIVE_DEV + ranks[j]
 
     def drain(index, carry):
         send(me, index, own_x_sem.at[index], mate).wait_send()
@@ -442,7 +473,8 @@
     f32, dma = jnp.float32, pltpu.SemaphoreType.DMA
     scratch = [
         pltpu.VMEM((SWEEPS * LIVE_DEV, depth + 16, sites), f32),
-        pltpu.VMEM((reps * LIVE_DEV, 2, depth, sites // 2), f32),
+        *[pltpu.VMEM((rep_dev, depth, sites), f32)] * SWEEPS,
+        *[pltpu.VMEM((2, depth, sites // 2), f32)] * LIVE_DEV,
         pltpu.VMEM((SWEEPS, 2, LIVE_DEV, 1, sites), f32),
         pltpu.VMEM((SWEEPS, 2, LIVE_DEV, 1, sites), f32),
         pltpu.VMEM((LIVE_DEV, depth * CHUNKS, 128), f32),
@@ -468,22 +500,56 @@
         dma((gzs,)),
         dma((reps,)),
         dma((reps,)),
+        dma((SWEEPS,)),
+        dma((LIVE_DEV,)),
     ]
     smem = pl.BlockSpec(memory_space=pltpu.SMEM)
     vmem = pl.BlockSpec(memory_space=pltpu.VMEM)
+    hbm = pl.BlockSpec(memory_space=pl.ANY)
+    gathered, chosen, propagator = pl.pallas_call(
+        functools.partial(kernel, reps, gzs, rep_dev),
+        out_shape=(
+            jax.ShapeDtypeStruct((reps * LIVE_DEV, 2, depth, sites // 2), f32),
+            jax.ShapeDtypeStruct((rep_dev,), jnp.int32),
+            jax.ShapeDtypeStruct((rep_dev, NBINS), f32),
+        ),
+        in_specs=[smem, smem, vmem, hbm, vmem, vmem, vmem, vmem, vmem],
+        out_specs=(hbm, smem, vmem),
+        scratch_shapes=scratch,
+        compiler_params=pltpu.CompilerParams(
+            collective_id=0, has_side_effects=True, vmem_limit_bytes=56 * 1024 * 1024
+        ),
+    )(
+        counts, dest_slots, lattice_field, langevin_noise, masses,
+        jnp.transpose(mode_bins, (2, 0, 1)), *map(jnp.asarray, tables()),
+    )
     return pl.pallas_call(
-        functools.partial(kernel, reps, gzs, rep_dev),
+        pick,
         out_shape=(
             jax.ShapeDtypeStruct(lattice_field.shape, f32),
             jax.ShapeDtypeStruct((rep_dev, NBINS), f32),
         ),
-        in_specs=[smem, smem] + [vmem] * 7,
-        out_specs=(vmem, vmem),
-        scratch_shapes=scratch,
-        compiler_params=pltpu.CompilerParams(
-            collective_id=0, has_side_effects=True, vmem_limit_bytes=56 * 1024 * 1024
+        grid_spec=pltpu.PrefetchScalarGridSpec(
+            num_scalar_prefetch=1,
+            grid=(rep_dev,),
+            in_specs=[
+                pl.BlockSpec((1, 2, depth, sites // 2), lambda j, chosen: (chosen[j], 0, 0, 0)),
+                pl.BlockSpec((rep_dev, NBINS), lambda j, chosen: (0, 0)),
+            ],
+            out_specs=(
+                pl.BlockSpec((1, depth, sites), lambda j, chosen: (j, 0, 0)),
+                pl.BlockSpec((rep_dev, NBINS), lambda j, chosen: (0, 0)),
+            ),
         ),
-    )(counts, dest_slots, lattice_field, langevin_noise, masses, mode_bins, *map(jnp.asarray, tables()))
+        compiler_params=pltpu.CompilerParams(vmem_limit_bytes=16 * 1024 * 1024),
+    )(chosen, gathered, propagator)
+
+
+def pick(chosen, slab, prop, out, prop_out):
+    half = slab.shape[3]
+    out[0, :, :half] = slab[0, 0]
+    out[0, :, half:] = slab[0, 1]
+    prop_out[...] = prop[...]
 
 
 def solution(mesh):

time: 93 us -> 90 us (0.968)
  Pallas kernels: 87 us -> 85 us
  local copies, waits for them, and re-layouts: 5.23 us -> 4.14 us
    pallas_call x1, Pallas kernels: 87 us -> 82.2 us  [local(): pl.pallas_call(functools.partial(kernel, reps, gzs, rep_dev), out_shape=(...]
    pallas_call x0 -> x1, Pallas kernels: none -> 2.82 us  [local(): pl.pallas_call(pick, out_shape=(jax.ShapeDtypeStruct(lattice_field.shape,...]
    unnamed x5 -> x6, local copies, waits for them, and re-layouts: 5.23 us -> 4.14 us
where the time goes in v4:
time: 90 us; the launch traced here: 89.8 us
  Pallas kernels  85 us (94%)
  local copies, waits for them, and re-layouts  4.14 us (5%)
    pallas_call x1, Pallas kernels, local(): pl.pallas_call(functools.partial(kernel, reps, gzs, rep_dev), out_shape=(...  82.2 us
    unnamed x6, local copies, waits for them, and re-layouts  4.14 us
    pallas_call x1, Pallas kernels, local(): pl.pallas_call(pick, out_shape=(jax.ShapeDtypeStruct(lattice_field.shape,...  2.82 us

profile of v4, /device:TPU:0, one launch (start us, length us, event | category | flops | bytes accessed | tf_op | source)
XLA Modules:
  0.0 89.8 jit_solution(15169654920908802010)
XLA Ops:
  0.6 82.2 %shard_map.104 = (f32[24,2,16,2048]{3,2,1,0:T(8,128)}, s32[6]{0:T(128)}, f32[6,16]{1,0:T(8,128)}) custom-call(s32[48]{0:T(128)} %counts.1, s32[48]{0:T(128)} %dest.1, f32[6,16,4096]{2,1,0:T(8,128)} %field.1, f32[2,6,16,4096]{3,2,1,0:T(8,128)} %noise_in.1, f32[16,4096]{1,0:T(8,128)} %masses.1, s32[33,16,64]{2,1,0:T(8,128)} %bitcast.1, ...), custom_call_target="tpu_custom_call" | custom-call | tf_op jit(solution)/shard_map/pallas_call | solution.py:509
  82.8 0.0 copy-start
  82.8 2.8 %copy-done = f32[24,2,16,2048]{3,2,1,0:T(8,128)S(1)} copy-done((f32[24,2,16,2048]{3,2,1,0:T(8,128)S(1)}, f32[24,2,16,2048]{3,2,1,0:T(8,128)}, u32[]{:S(2)}) %copy-start) | copy-done | bytes 6291480
  85.6 0.0 copy-start.1
  85.6 0.7 copy-done.1
  86.3 0.0 copy-start.2
  86.3 0.7 copy-done.2
  86.9 2.8 %shard_map.105 = (f32[6,16,4096]{2,1,0:T(8,128)}, f32[6,16]{1,0:T(8,128)}) custom-call(s32[6]{0:T(128)S(1)} %copy-done.2, f32[24,2,16,2048]{3,2,1,0:T(8,128)S(1)} %copy-done, f32[6,16]{1,0:T(8,128)S(1)} %copy-done.1), custom_call_target="tpu_custom_call" | custom-call | tf_op jit(solution)/shard_map/pallas_call | solution.py:526
Async XLA Ops:
  82.8 2.8 %copy-start = (f32[24,2,16,2048]{3,2,1,0:T(8,128)S(1)}, f32[24,2,16,2048]{3,2,1,0:T(8,128)}, u32[]{:S(2)}) copy-start(f32[24,2,16,2048]{3,2,1,0:T(8,128)} %get-tuple-element.6.slab) | copy-start | bytes 18874372
  85.6 0.7 copy-start.1
  86.3 0.7 copy-start.2

commit v5 on v4

--- a/solution.py
+++ b/solution.py
@@ -529,27 +529,24 @@
             jax.ShapeDtypeStruct(lattice_field.shape, f32),
             jax.ShapeDtypeStruct((rep_dev, NBINS), f32),
         ),
-        grid_spec=pltpu.PrefetchScalarGridSpec(
-            num_scalar_prefetch=1,
-            grid=(rep_dev,),
-            in_specs=[
-                pl.BlockSpec((1, 2, depth, sites // 2), lambda j, chosen: (chosen[j], 0, 0, 0)),
-                pl.BlockSpec((rep_dev, NBINS), lambda j, chosen: (0, 0)),
-            ],
-            out_specs=(
-                pl.BlockSpec((1, depth, sites), lambda j, chosen: (j, 0, 0)),
-                pl.BlockSpec((rep_dev, NBINS), lambda j, chosen: (0, 0)),
-            ),
-        ),
-        compiler_params=pltpu.CompilerParams(vmem_limit_bytes=16 * 1024 * 1024),
+        in_specs=[smem, hbm, hbm],
+        out_specs=(hbm, hbm),
+        scratch_shapes=[dma((2 * rep_dev + 1,))],
+        compiler_params=pltpu.CompilerParams(vmem_limit_bytes=56 * 1024 * 1024),
     )(chosen, gathered, propagator)
 
 
-def pick(chosen, slab, prop, out, prop_out):
-    half = slab.shape[3]
-    out[0, :, :half] = slab[0, 0]
-    out[0, :, half:] = slab[0, 1]
-    prop_out[...] = prop[...]
+def pick(chosen, gathered, prop, out, prop_out, sem):
+    rep_dev, half = out.shape[0], gathered.shape[3]
+    copies = [pltpu.make_async_copy(prop, prop_out, sem.at[2 * rep_dev])]
+    for j in range(rep_dev):
+        for h in range(2):
+            target = out.at[j, :, half * h : half * h + half]
+            copies.append(pltpu.make_async_copy(gathered.at[chosen[j], h], target, sem.at[2 * j + h]))
+    for copy in copies:
+        copy.start()
+    for copy in copies:
+        copy.wait()
 
 
 def solution(mesh):

time: 90 us -> 133 us (1.48)
  Pallas kernels: 85 us -> 132 us
  local copies, waits for them, and re-layouts: 4.14 us -> 0 us
    pallas_call x1, Pallas kernels: 2.82 us -> 49.6 us  [local(): pl.pallas_call(pick, out_shape=(jax.ShapeDtypeStruct(lattice_field.shape,...]
    unnamed x6 -> x0, local copies, waits for them, and re-layouts: 4.14 us -> none
where the time goes in v5:
time: 133 us; the launch traced here: 132 us
  Pallas kernels  132 us (99%)
    pallas_call x1, Pallas kernels, local(): pl.pallas_call(functools.partial(kernel, reps, gzs, rep_dev), out_shape=(...  82.1 us
    pallas_call x1, Pallas kernels, local(): pl.pallas_call(pick, out_shape=(jax.ShapeDtypeStruct(lattice_field.shape,...  49.6 us

profile of v5, /device:TPU:0, one launch (start us, length us, event | category | flops | bytes accessed | tf_op | source)
XLA Modules:
  0.0 132.4 jit_solution(10491365204866091953)
XLA Ops:
  0.6 82.1 %shard_map.104 = (f32[24,2,16,2048]{3,2,1,0:T(8,128)}, s32[6]{0:T(128)}, f32[6,16]{1,0:T(8,128)}) custom-call(s32[48]{0:T(128)} %counts.1, s32[48]{0:T(128)} %dest.1, f32[6,16,4096]{2,1,0:T(8,128)} %field.1, f32[2,6,16,4096]{3,2,1,0:T(8,128)} %noise_in.1, f32[16,4096]{1,0:T(8,128)} %masses.1, s32[33,16,64]{2,1,0:T(8,128)} %bitcast.1, ...), custom_call_target="tpu_custom_call" | custom-call | tf_op jit(solution)/shard_map/pallas_call | solution.py:509
  82.8 49.6 %shard_map.105 = (f32[6,16,4096]{2,1,0:T(8,128)}, f32[6,16]{1,0:T(8,128)}) custom-call(s32[6]{0:T(128)} %get-tuple-element.5.chosen, f32[24,2,16,2048]{3,2,1,0:T(8,128)} %get-tuple-element.6.gathered, f32[6,16]{1,0:T(8,128)} %get-tuple-element.7.prop), custom_call_target="tpu_custom_call" | custom-call | tf_op jit(solution)/shard_map/pallas_call | solution.py:526

commit v6 on v5

--- a/solution.py
+++ b/solution.py
@@ -531,22 +531,32 @@
         ),
         in_specs=[smem, hbm, hbm],
         out_specs=(hbm, hbm),
-        scratch_shapes=[dma((2 * rep_dev + 1,))],
+        scratch_shapes=[
+            pltpu.VMEM((rep_dev, 2, depth, sites // 2), f32),
+            pltpu.VMEM((rep_dev, NBINS), f32),
+            dma((2 * rep_dev + 1,)),
+            dma((2 * rep_dev + 1,)),
+        ],
         compiler_params=pltpu.CompilerParams(vmem_limit_bytes=56 * 1024 * 1024),
     )(chosen, gathered, propagator)
 
 
-def pick(chosen, gathered, prop, out, prop_out, sem):
+def pick(chosen, gathered, prop, out, prop_out, held, held_prop, in_sem, out_sem):
     rep_dev, half = out.shape[0], gathered.shape[3]
-    copies = [pltpu.make_async_copy(prop, prop_out, sem.at[2 * rep_dev])]
+    loads = [pltpu.make_async_copy(prop, held_prop, in_sem.at[2 * rep_dev])]
+    stores = [pltpu.make_async_copy(held_prop, prop_out, out_sem.at[2 * rep_dev])]
     for j in range(rep_dev):
         for h in range(2):
-            target = out.at[j, :, half * h : half * h + half]
-            copies.append(pltpu.make_async_copy(gathered.at[chosen[j], h], target, sem.at[2 * j + h]))
-    for copy in copies:
-        copy.start()
-    for copy in copies:
-        copy.wait()
+            lanes, at = slice(half * h, half * h + half), 2 * j + h
+            loads.append(pltpu.make_async_copy(gathered.at[chosen[j], h], held.at[j, h], in_sem.at[at]))
+            stores.append(pltpu.make_async_copy(held.at[j, h], out.at[j, :, lanes], out_sem.at[at]))
+    for load in loads:
+        load.start()
+    for load, store in zip(loads, stores):
+        load.wait()
+        store.start()
+    for store in stores:
+        store.wait()
 
 
 def solution(mesh):

time: 133 us -> 86 us (0.65)
  Pallas kernels: 132 us -> 85.2 us
    pallas_call x1, Pallas kernels: 49.6 us -> 3.01 us  [local(): pl.pallas_call(pick, out_shape=(jax.ShapeDtypeStruct(lattice_field.shape,...]
where the time goes in v6:
time: 86 us; the launch traced here: 85.8 us
  Pallas kernels  85.2 us (99%)
    pallas_call x1, Pallas kernels, local(): pl.pallas_call(functools.partial(kernel, reps, gzs, rep_dev), out_shape=(...  82.1 us
    pallas_call x1, Pallas kernels, local(): pl.pallas_call(pick, out_shape=(jax.ShapeDtypeStruct(lattice_field.shape,...  3.01 us

profile of v6, /device:TPU:0, one launch (start us, length us, event | category | flops | bytes accessed | tf_op | source)
XLA Modules:
  0.0 85.8 jit_solution(11614502751807759151)
XLA Ops:
  0.6 82.1 %shard_map.104 = (f32[24,2,16,2048]{3,2,1,0:T(8,128)}, s32[6]{0:T(128)}, f32[6,16]{1,0:T(8,128)}) custom-call(s32[48]{0:T(128)} %counts.1, s32[48]{0:T(128)} %dest.1, f32[6,16,4096]{2,1,0:T(8,128)} %field.1, f32[2,6,16,4096]{3,2,1,0:T(8,128)} %noise_in.1, f32[16,4096]{1,0:T(8,128)} %masses.1, s32[33,16,64]{2,1,0:T(8,128)} %bitcast.1, ...), custom_call_target="tpu_custom_call" | custom-call | tf_op jit(solution)/shard_map/pallas_call | solution.py:509
  82.8 3.0 %shard_map.105 = (f32[6,16,4096]{2,1,0:T(8,128)}, f32[6,16]{1,0:T(8,128)}) custom-call(s32[6]{0:T(128)} %get-tuple-element.5.chosen, f32[24,2,16,2048]{3,2,1,0:T(8,128)} %get-tuple-element.6.gathered, f32[6,16]{1,0:T(8,128)} %get-tuple-element.7.prop), custom_call_target="tpu_custom_call" | custom-call | tf_op jit(solution)/shard_map/pallas_call | solution.py:526
